TPU v7x, 32 devices: a whole 2x2x4 slice. The times are simulated.
32 devices in a mesh: sx: 4 (over x, core), sy: 4 (over z), depth: 2 (over y).
Axes of the slice: x: 2, y: 2, z: 4, core: 2. Of those that a mesh axis runs over, the one named last changes fastest.
Arguments:
- probe_wave: float32 [2, 128, 128], replicated, may hold values from -4.2 to 4.2
- transmission: float32 [2, 8, 512, 1024], P(None, 'depth', 'sx', 'sy'), may hold values from -0.6 to 0.6
- scan_offsets: int32 [4, 4, 4, 2], P('sx', 'sy'), may hold values from -64 to 192, as said below
- pattern_shifts: int32 [4, 4, 4, 2], P('sx', 'sy'), may hold values from -8 to 8
- patterns: float32 [4, 4, 4, 128, 128], P('sx', 'sy'), may hold values from 0 to 9
Outputs:
- transmission_grad: float32 [2, 8, 512, 1024], P(None, 'depth', 'sx', 'sy')
- probe_grad: float32 [2, 128, 128], replicated
- mean_error: float32 [], replicated
Inputs may be any that keep to these rules, and one draw needn't show every extreme that they name: `scan_offsets`: row offsets lie from -64 to 64 and column offsets from -64 to 192; on every scan tile some position takes the smallest and some the largest value of each.
All inputs are finite; a program needn't handle non-finite values.
Results may differ from a plain program's by a relative error of at most 0.0003.
Values sent between devices are 32-bit elements; how exact they have to be, the bound alone decides.
A program may use at most 64 MiB of HBM per device.

v0:
```python
import jax
import jax.numpy as jnp
from jax import lax
from jax.sharding import PartitionSpec as P

FRESNEL = 12.0
PRECISE = lax.Precision.HIGHEST


def with_halo(shard, sides, width):
    for axis, dim in sides:
        size, length = (lax.axis_size(axis), shard.shape[dim])
        up = [(i, (i + 1) % size) for i in range(size - 1)]
        down = [(j, i) for i, j in up]
        last = lax.slice_in_dim(shard, length - width, length, axis=dim)
        first = lax.slice_in_dim(shard, 0, width, axis=dim)
        before = lax.ppermute(last, axis, up)
        after = lax.ppermute(first, axis, down)
        shard = jnp.concatenate([before, shard, after], axis=dim)
    return shard


def from_behind(value, axis, steps):
    count = lax.axis_size(axis)
    first, last = (max(0, -steps), min(count, count - steps))
    return lax.ppermute(value, axis, [(source, source + steps) for source in range(first, last)])


def build_tables(points):
    counter = jnp.arange(points, dtype=jnp.int32)
    angles = (counter[:, None] * counter[None, :] % points).astype(jnp.float32) * (
        2.0 * jnp.pi / points
    )
    factor = 1.0 / jnp.sqrt(jnp.float32(points))
    fourier_real = jnp.cos(angles) * factor
    fourier_imag = -jnp.sin(angles) * factor
    frequency = (
        jnp.where(counter < points // 2, counter, counter - points).astype(jnp.float32) / points
    )
    phases = -FRESNEL * frequency * frequency
    kernel_real = jnp.cos(phases)
    kernel_imag = jnp.sin(phases)
    left_real = fourier_real * kernel_real[None, :] + fourier_imag * kernel_imag[None, :]
    left_imag = fourier_real * kernel_imag[None, :] - fourier_imag * kernel_real[None, :]
    prop_real = jnp.dot(left_real, fourier_real, precision=PRECISE) - jnp.dot(
        left_imag, fourier_imag, precision=PRECISE
    )
    prop_imag = jnp.dot(left_real, fourier_imag, precision=PRECISE) + jnp.dot(
        left_imag, fourier_real, precision=PRECISE
    )
    return ((fourier_real, fourier_imag), (prop_real, prop_imag))


def conjugate(matrix):
    return (matrix[0], -matrix[1])


def left_apply(matrix, fields):
    matrix_real, matrix_imag = matrix
    field_real = fields[:, 0]
    field_imag = fields[:, 1]
    product_real = jnp.einsum(
        "ij,njk->nik", matrix_real, field_real, precision=PRECISE
    ) - jnp.einsum("ij,njk->nik", matrix_imag, field_imag, precision=PRECISE)
    product_imag = jnp.einsum(
        "ij,njk->nik", matrix_real, field_imag, precision=PRECISE
    ) + jnp.einsum("ij,njk->nik", matrix_imag, field_real, precision=PRECISE)
    return jnp.stack([product_real, product_imag], axis=1)


def right_apply(fields, matrix):
    matrix_real, matrix_imag = matrix
    field_real = fields[:, 0]
    field_imag = fields[:, 1]
    product_real = jnp.einsum(
        "nij,jk->nik", field_real, matrix_real, precision=PRECISE
    ) - jnp.einsum("nij,jk->nik", field_imag, matrix_imag, precision=PRECISE)
    product_imag = jnp.einsum(
        "nij,jk->nik", field_imag, matrix_real, precision=PRECISE
    ) + jnp.einsum("nij,jk->nik", field_real, matrix_imag, precision=PRECISE)
    return jnp.stack([product_real, product_imag], axis=1)


def apply_both(matrix, fields):
    return right_apply(left_apply(matrix, fields), matrix)


def complex_times(former, latter):
    return jnp.stack(
        [
            former[:, 0] * latter[:, 0] - former[:, 1] * latter[:, 1],
            former[:, 0] * latter[:, 1] + former[:, 1] * latter[:, 0],
        ],
        axis=1,
    )


def conj_times(former, latter):
    return jnp.stack(
        [
            former[:, 0] * latter[:, 0] + former[:, 1] * latter[:, 1],
            former[:, 0] * latter[:, 1] - former[:, 1] * latter[:, 0],
        ],
        axis=1,
    )


def slab_factor(windows, slab_number):
    slab_tile = windows[:, :, slab_number]
    return jnp.stack([1.0 + slab_tile[:, 0], slab_tile[:, 1]], axis=1)


def forward_section(current, windows, propagator):
    incident_list = []
    for slab_number in range(windows.shape[2]):
        incident_list.append(current)
        current = apply_both(propagator, complex_times(current, slab_factor(windows, slab_number)))
    return (current, jnp.stack(incident_list, axis=1))


def backward_section(gradient, windows, incident, propagator):
    back_prop = conjugate(propagator)
    slab_total = windows.shape[2]
    pieces = [None] * slab_total
    for slab_number in reversed(range(slab_total)):
        gradient = apply_both(back_prop, gradient)
        pieces[slab_number] = conj_times(incident[:, slab_number], gradient)
        gradient = conj_times(slab_factor(windows, slab_number), gradient)
    return (gradient, jnp.stack(pieces, axis=2))


def detector(leaving, measured, shifts, fourier):
    points = leaving.shape[-1]
    farfield = apply_both(fourier, leaving)
    intensity = farfield[:, 0] ** 2 + farfield[:, 1] ** 2
    counter = jnp.arange(points, dtype=jnp.int32)
    row_perm = (
        counter[None, None, :] == (counter[None, :, None] - shifts[:, 0, None, None]) % points
    ).astype(jnp.float32)
    col_perm = (
        counter[None, None, :] == (counter[None, :, None] - shifts[:, 1, None, None]) % points
    ).astype(jnp.float32)
    moved = jnp.einsum("nua,nav->nuv", row_perm, intensity, precision=PRECISE)
    moved = jnp.einsum("nuc,nvc->nuv", moved, col_perm, precision=PRECISE)
    residual = moved - measured
    total_error = 0.5 * jnp.sum(residual * residual)
    pulled = jnp.einsum("nua,nuv->nav", row_perm, residual, precision=PRECISE)
    pulled = jnp.einsum("nav,nvc->nac", pulled, col_perm, precision=PRECISE)
    grad_far = 2.0 * pulled[:, None] * farfield
    return (total_error, apply_both(conjugate(fourier), grad_far))


def cut_windows(padded, anchors, points):

    def single(anchor_pair):
        zero_index = jnp.zeros((), jnp.int32)
        return lax.dynamic_slice(
            padded,
            (zero_index, zero_index, anchor_pair[0], anchor_pair[1]),
            (padded.shape[0], padded.shape[1], points, points),
        )

    return jax.vmap(single)(anchors)


def add_windows(gradient_ext, anchors, pieces):

    def add_one(number, accumulated):
        zero_index = jnp.zeros((), jnp.int32)
        corner = (zero_index, zero_index, anchors[number, 0], anchors[number, 1])
        current = lax.dynamic_slice(accumulated, corner, pieces.shape[1:])
        return lax.dynamic_update_slice(accumulated, current + pieces[number], corner)

    return lax.fori_loop(0, pieces.shape[0], add_one, gradient_ext)


def fold_rims(folded, border, row_count, col_count):
    inner = 2 * border
    lower_start = row_count + 3 * border
    right_start = col_count + 3 * border
    center = folded[:, :, inner : row_count + inner, inner : col_count + inner]
    center = center.at[:, :, :border, :].add(folded[:, :, :border, inner : col_count + inner])
    center = center.at[:, :, row_count - border :, :].add(
        folded[:, :, lower_start:, inner : col_count + inner]
    )
    center = center.at[:, :, :, :border].add(folded[:, :, inner : row_count + inner, :border])
    center = center.at[:, :, :, col_count - border :].add(
        folded[:, :, inner : row_count + inner, right_start:]
    )
    center = center.at[:, :, :border, :border].add(folded[:, :, :border, :border])
    center = center.at[:, :, :border, col_count - border :].add(folded[:, :, :border, right_start:])
    center = center.at[:, :, row_count - border :, :border].add(folded[:, :, lower_start:, :border])
    center = center.at[:, :, row_count - border :, col_count - border :].add(
        folded[:, :, lower_start:, right_start:]
    )
    return center


def local(probe_wave, transmission, scan_offsets, pattern_shifts, patterns):
    points = probe_wave.shape[-1]
    border = points // 2
    slab_count = transmission.shape[1]
    row_count = transmission.shape[2]
    col_count = transmission.shape[3]
    fourier, propagator = build_tables(points)
    padded = with_halo(transmission, (("sx", 2), ("sy", 3)), border)
    anchors = scan_offsets.reshape(-1, 2) + border
    shifts_all = pattern_shifts.reshape(-1, 2)
    measured = patterns.reshape(-1, points, points)
    positions = anchors.shape[0]
    depth_count = lax.axis_size("depth")
    depth_index = lax.axis_index("depth")
    last_section = depth_count - 1
    batch_count = 1
    per_group = positions // batch_count
    rounds = depth_count + batch_count - 1
    wave_shape = (per_group, 2, points, points)
    incident_store = jnp.zeros((positions, slab_count, 2, points, points), jnp.float32)
    exit_store = jnp.zeros((positions, 2, points, points), jnp.float32)
    incoming = jnp.zeros(wave_shape, jnp.float32)
    probe_batch = jnp.broadcast_to(probe_wave[None], wave_shape)
    for round_number in range(rounds):
        group_index = round_number - depth_index
        active = (group_index >= 0) & (group_index < batch_count)
        group_anchors = anchors
        windows = cut_windows(padded, group_anchors, points)
        entering = jnp.where(depth_index == 0, probe_batch, incoming)
        leaving, incident = forward_section(entering, windows, propagator)
        old_incident = incident_store
        incident_store = jnp.where(active, incident, old_incident)
        old_exit = exit_store
        exit_store = jnp.where(active, leaving, old_exit)
        if round_number + 1 < rounds:
            incoming = from_behind(leaving, "depth", 1)
    error_part, grad_exits = detector(exit_store, measured, shifts_all, fourier)
    error_part = jnp.where(depth_index == last_section, error_part, 0.0)
    gradient_ext = jnp.zeros(padded.shape, jnp.float32)
    probe_part = jnp.zeros((2, points, points), jnp.float32)
    incoming = jnp.zeros(wave_shape, jnp.float32)
    for round_number in range(rounds):
        group_index = round_number - (last_section - depth_index)
        active = (group_index >= 0) & (group_index < batch_count)
        group_anchors = anchors
        windows = cut_windows(padded, group_anchors, points)
        entering = jnp.where(depth_index == last_section, grad_exits, incoming)
        incident = incident_store
        grad_start, pieces = backward_section(entering, windows, incident, propagator)
        weight = active.astype(jnp.float32)
        gradient_ext = add_windows(gradient_ext, group_anchors, pieces * weight)
        probe_part = probe_part + jnp.where(
            active & (depth_index == 0), jnp.sum(grad_start, axis=0), 0.0
        )
        if round_number + 1 < rounds:
            incoming = from_behind(grad_start, "depth", -1)
    totals = lax.psum((probe_part, error_part), ("sx", "sy", "depth"))
    folded = with_halo(gradient_ext, (("sx", 2), ("sy", 3)), border)
    transmission_grad = fold_rims(folded, border, row_count, col_count)
    all_positions = positions * lax.axis_size("sx") * lax.axis_size("sy")
    probe_grad = totals[0] / all_positions
    mean_error = totals[1] / (all_positions * points * points)
    return (transmission_grad, probe_grad, mean_error)


def solution(mesh):
    in_specs = (
        P(),
        P(None, "depth", "sx", "sy"),
        P("sx", "sy", None, None),
        P("sx", "sy", None, None),
        P("sx", "sy", None, None, None),
    )
    out_specs = (P(None, "depth", "sx", "sy"), P(), P())
    return jax.shard_map(local, mesh=mesh, in_specs=in_specs, out_specs=out_specs, check_vma=False)
```

profile of v0, /device:TPU:0, one launch (start us, length us, event | category | flops | bytes accessed | tf_op | source)
XLA Modules:
  0.0 462.5 jit_solution(47410691369960203)
XLA Ops:
  20.6 4.3 collective-permute-start.2
  27.5 3.7 collective-permute-done.2
  31.1 5.2 %collective-permute-done.3 = f32[2,4,256,64]{2,3,1,0:T(8,128)} collective-permute-done((f32[2,4,256,64]{2,3,1,0:T(8,128)}, f32[2,4,256,64]{2,3,1,0:T(8,128)}, u32[]{:S(2)}, u32[]{:S(2)}) %collective-permute-start.3) | collective-permute-done | bytes 524320 | tf_op jit(solution)/shard_map/ppermute | solution.py:18
  36.3 3.7 pad_maximum_fusion
  40.1 17.8 %while.37 = (s32[]{:T(128)}, f32[2,4,256,384]{2,3,1,0:T(8,128)}, s32[4,4]{1,0:T(4,128)S(1)}, f32[4,2,4,128,128]{4,3,0,1,2:T(8,128)}, s32[]{:T(128)}) while((s32[]{:T(128)}, f32[2,4,256,384]{2,3,1,0:T(8,128)}, s32[4,4]{1,0:T(4,128)S(1)}, f32[4,2,4,128,128]{4,3,0,1,2:T(8,128)}, s32[]{:T(128)}) %tuple.184), condition=%wide.while_cond.8, body=%wide.while_body.8.sunk | while | flops 2 | bytes 3145861 | solution.py:157
  40.7 2.6 constant_dynamic-slice_fusion.21
  44.9 2.7 constant_dynamic-slice_fusion.21
  49.4 2.7 constant_dynamic-slice_fusion.21
  53.8 2.7 constant_dynamic-slice_fusion.21
  79.4 3.6 collective-permute-start.4
  83.2 7.0 %collective-permute-done.4 = f32[4,2,128,128]{3,2,0,1:T(8,128)S(1)} collective-permute-done((f32[4,2,128,128]{3,2,0,1:T(8,128)S(1)}, f32[4,2,128,128]{3,2,0,1:T(8,128)S(1)}, u32[]{:S(2)}, u32[]{:S(2)}) %collective-permute-start.4) | collective-permute-done | bytes 524320 | tf_op jit(solution)/shard_map/ppermute | solution.py:26
  147.8 9.7 %collective-permute-done.5 = f32[4,2,128,128]{3,2,0,1:T(8,128)S(1)} collective-permute-done((f32[4,2,128,128]{3,2,0,1:T(8,128)S(1)}, f32[4,2,128,128]{3,2,0,1:T(8,128)S(1)}, u32[]{:S(2)}, u32[]{:S(2)}) %collective-permute-start.5) | collective-permute-done | bytes 524320 | tf_op jit(solution)/shard_map/ppermute | solution.py:26
  182.4 50.1 %while.35 = (s32[]{:T(128)}, f32[2,4,256,384]{3,2,1,0:T(8,128)S(1)}, s32[4,2]{0,1:T(2,128)S(1)}, f32[4,2,4,128,128]{4,3,0,1,2:T(8,128)}, s32[]{:T(128)}, /*index=5*/s32[]{:T(128)}, s32[]{:T(128)}, s32[]{:T(128)}) while((s32[]{:T(128)}, f32[2,4,256,384]{3,2,1,0:T(8,128)S(1)}, s32[4,2]{0,1:T(2,128)S(1)}, f32[4,2,4,128,128]{4,3,0,1,2:T(8,128)}, ...), condition=%wide.region_1.2_spmd, body=%wide.region_0.1_spmd.sunk | while | flops 131080 | bytes 2621637 | solution.py:174
  188.9 4.6 dynamic_update_slice.16
  200.0 7.1 %dynamic_update_slice.16 = f32[2,4,256,384]{3,2,1,0:T(8,128)S(1)} dynamic-update-slice(f32[2,4,256,384]{3,2,1,0:T(8,128)S(1)} %get-tuple-element.550, f32[2,4,128,128]{3,2,1,0:T(8,128)} %fusion.585, s32[]{:T(128)} %constant.342.clone.1..sunk, s32[]{:T(128)} %constant.342.clone.1..sunk, s32[]{:T(128)S(6)} %select_n.363, s32[]{:T(128)S(6)} %select_n.364) | dynamic-update-slice | bytes 1048580 | tf_op jit(solution)/shard_map/while/body/eval_jaxpr/dynamic_update_slice | solution.py:172
  213.7 6.9 %dynamic_update_slice.16 = f32[2,4,256,384]{3,2,1,0:T(8,128)S(1)} dynamic-update-slice(f32[2,4,256,384]{3,2,1,0:T(8,128)S(1)} %get-tuple-element.550, f32[2,4,128,128]{3,2,1,0:T(8,128)} %fusion.585, s32[]{:T(128)} %constant.342.clone.1..sunk, s32[]{:T(128)} %constant.342.clone.1..sunk, s32[]{:T(128)S(6)} %select_n.363, s32[]{:T(128)S(6)} %select_n.364) | dynamic-update-slice | bytes 1048580 | tf_op jit(solution)/shard_map/while/body/eval_jaxpr/dynamic_update_slice | solution.py:172
  227.1 5.4 %dynamic_update_slice.16 = f32[2,4,256,384]{3,2,1,0:T(8,128)S(1)} dynamic-update-slice(f32[2,4,256,384]{3,2,1,0:T(8,128)S(1)} %get-tuple-element.550, f32[2,4,128,128]{3,2,1,0:T(8,128)} %fusion.585, s32[]{:T(128)} %constant.342.clone.1..sunk, s32[]{:T(128)} %constant.342.clone.1..sunk, s32[]{:T(128)S(6)} %select_n.363, s32[]{:T(128)S(6)} %select_n.364) | dynamic-update-slice | bytes 1048580 | tf_op jit(solution)/shard_map/while/body/eval_jaxpr/dynamic_update_slice | solution.py:172
  236.4 49.1 %while.36 = (s32[]{:T(128)}, f32[2,4,256,384]{3,2,1,0:T(8,128)S(1)}, s32[4,2]{0,1:T(2,128)S(1)}, f32[4,2,4,128,128]{4,3,0,1,2:T(8,128)}, s32[]{:T(128)}, /*index=5*/s32[]{:T(128)}, s32[]{:T(128)}, s32[]{:T(128)}) while((s32[]{:T(128)}, f32[2,4,256,384]{3,2,1,0:T(8,128)S(1)}, s32[4,2]{0,1:T(2,128)S(1)}, f32[4,2,4,128,128]{4,3,0,1,2:T(8,128)}, ...), condition=%wide.region_3.4_spmd, body=%wide.region_2.3_spmd.sunk | while | flops 131080 | bytes 2621637 | solution.py:174
  242.7 4.6 dynamic_update_slice.17
  253.5 7.1 %dynamic_update_slice.17 = f32[2,4,256,384]{3,2,1,0:T(8,128)S(1)} dynamic-update-slice(f32[2,4,256,384]{3,2,1,0:T(8,128)S(1)} %get-tuple-element.574, f32[2,4,128,128]{3,2,1,0:T(8,128)} %fusion.586, s32[]{:T(128)} %constant.342.clone.1..sunk.1, s32[]{:T(128)} %constant.342.clone.1..sunk.1, s32[]{:T(128)S(6)} %select_n.365, s32[]{:T(128)S(6)} %select_n.366) | dynamic-update-slice | bytes 1048580 | tf_op jit(solution)/shard_map/while/body/eval_jaxpr/dynamic_update_slice | solution.py:172
  266.9 6.9 %dynamic_update_slice.17 = f32[2,4,256,384]{3,2,1,0:T(8,128)S(1)} dynamic-update-slice(f32[2,4,256,384]{3,2,1,0:T(8,128)S(1)} %get-tuple-element.574, f32[2,4,128,128]{3,2,1,0:T(8,128)} %fusion.586, s32[]{:T(128)} %constant.342.clone.1..sunk.1, s32[]{:T(128)} %constant.342.clone.1..sunk.1, s32[]{:T(128)S(6)} %select_n.365, s32[]{:T(128)S(6)} %select_n.366) | dynamic-update-slice | bytes 1048580 | tf_op jit(solution)/shard_map/while/body/eval_jaxpr/dynamic_update_slice | solution.py:172
  280.2 5.4 %dynamic_update_slice.17 = f32[2,4,256,384]{3,2,1,0:T(8,128)S(1)} dynamic-update-slice(f32[2,4,256,384]{3,2,1,0:T(8,128)S(1)} %get-tuple-element.574, f32[2,4,128,128]{3,2,1,0:T(8,128)} %fusion.586, s32[]{:T(128)} %constant.342.clone.1..sunk.1, s32[]{:T(128)} %constant.342.clone.1..sunk.1, s32[]{:T(128)S(6)} %select_n.365, s32[]{:T(128)S(6)} %select_n.366) | dynamic-update-slice | bytes 1048580 | tf_op jit(solution)/shard_map/while/body/eval_jaxpr/dynamic_update_slice | solution.py:172
  288.2 8.8 %collective-permute-start.6 = (f32[2,4,64,384]{3,2,1,0:T(8,128)}, f32[2,4,64,384]{3,2,1,0:T(8,128)}, u32[]{:S(2)}, u32[]{:S(2)}) collective-permute-start(f32[2,4,64,384]{3,2,1,0:T(8,128)} %get-tuple-element.335), channel_id=1, source_target_pairs={{0,8},{8,16},{16,24},{1,9},{9,17},{17,25},{2,10},{10,18},{18,26},{... | collective-permute-start | bytes 2359304 | tf_op jit(solution)/shard_map/ppermute | solution.py:17
  302.5 2.8 copy.481
  305.2 2.8 copy.479
  308.0 3.3 pad_maximum_fusion.1
  313.3 42.4 %psum.15 = f32[]{:T(128)} all-reduce(f32[]{:T(128)S(6)} %select_n.244), channel_id=1, replica_groups=mesh['sx'=4,'sy'=4,'depth'=2] {'sx','sy','depth'}, use_global_device_ids=true, to_apply=%region_9.10 | all-reduce | flops 1 | bytes 8 | tf_op jit(solution)/shard_map/psum | solution.py:255
  357.7 4.6 collective-permute-start.8
  362.2 61.6 %all-reduce.2.cloned.1.call-done = f32[2,128,128]{2,1,0:T(8,128)} async-done(((f32[2,128,128]{2,1,0:T(8,128)}), f32[2,128,128]{2,1,0:T(8,128)}) %all-reduce.2.cloned.1.call-update) | async-done | bytes 131088 | tf_op jit(solution)/shard_map/psum | solution.py:255
  437.8 2.6 scatter-add.31
  443.7 4.9 %scatter-add.35 = f32[2,4,128,256]{3,2,1,0:T(8,128)S(1)} dynamic-update-slice(f32[2,4,128,256]{3,2,1,0:T(8,128)S(1)} %scatter-add.34, f32[2,4,64,64]{3,2,1,0:T(8,128)S(1)} %add_select_fusion, s32[]{:T(128)} %constant.342.clone.1, s32[]{:T(128)} %constant.342.clone.1, s32[]{:T(128)} %bitcast.142, s32[]{:T(128)} %bitcast.143) | dynamic-update-slice | bytes 262148 | tf_op jit(solution)/shard_map/scatter-add | solution.py:191
  449.8 3.5 scatter-add.39
  (309 shorter events, 180.6 us)
Async XLA Ops:
  7.2 6.8 %copy-start.2 = (f32[2,4,128,256]{3,2,1,0:T(8,128)S(1)}, f32[2,4,128,256]{3,2,1,0:T(8,128)}, u32[]{:S(2)}) copy-start(f32[2,4,128,256]{3,2,1,0:T(8,128)} %param.26) | copy-start | bytes 3145732
  7.2 6.0 %copy-start.13 = (s32[1,1,4,2]{2,3,1,0:T(2,128)S(1)}, s32[1,1,4,2]{2,3,1,0:T(2,128)}, u32[]{:S(2)}) copy-start(s32[1,1,4,2]{2,3,1,0:T(2,128)} %param.27) | copy-start | bytes 100
  7.2 6.8 %copy-start.14 = (s32[1,1,4,2]{2,3,1,0:T(2,128)S(1)}, s32[1,1,4,2]{2,3,1,0:T(2,128)}, u32[]{:S(2)}) copy-start(s32[1,1,4,2]{2,3,1,0:T(2,128)} %param.28) | copy-start | bytes 100
  7.2 416.6 %all-reduce.2.cloned.1.call-start = ((), (), s32[]{:S(2)}) async-start(), calls=%async_computation | async-start | bytes 262144 | tf_op jit(solution)/shard_map/psum | solution.py:255
  9.4 5.9 %collective-permute-start = (f32[2,4,64,256]{3,2,1,0:T(8,128)}, f32[2,4,64,256]{3,2,1,0:T(8,128)S(1)}, u32[]{:S(2)}, u32[]{:S(2)}) collective-permute-start(f32[2,4,64,256]{3,2,1,0:T(8,128)} %get-tuple-element.392), channel_id=1, source_target_pairs={{0,8},{8,16},{16,24},{1,9},{9,17},{17,25},{2,10},{10,18},{18,26},{... | collective-permute-start | bytes 1572872 | tf_op jit(solution)/shard_map/ppermute | solution.py:17
  11.8 6.0 %collective-permute-start.1 = (f32[2,4,64,256]{3,2,1,0:T(8,128)S(1)}, f32[2,4,64,256]{3,2,1,0:T(8,128)}, u32[]{:S(2)}, u32[]{:S(2)}) collective-permute-start(f32[2,4,64,256]{3,2,1,0:T(8,128)S(1)} %get-tuple-element.393), channel_id=1, source_target_pairs={{8,0},{16,8},{24,16},{9,1},{17,9},{25,17},{10,2},{18,10},{26,18},{... | collective-permute-start | bytes 1572872 | tf_op jit(solution)/shard_map/ppermute | solution.py:18
  19.2 7.6 %copy-start.3 = (f32[2,128,128]{2,1,0:T(8,128)S(1)}, f32[2,128,128]{2,1,0:T(8,128)}, u32[]{:S(2)}) copy-start(f32[2,128,128]{2,1,0:T(8,128)} %param.25) | copy-start | bytes 393220
  20.6 10.5 %collective-permute-start.2 = (f32[2,4,256,64]{2,3,1,0:T(8,128)}, f32[2,4,256,64]{2,3,1,0:T(8,128)}, u32[]{:S(2)}, u32[]{:S(2)}) collective-permute-start(f32[2,4,256,64]{2,3,1,0:T(8,128)} %get-tuple-element.336), channel_id=1, source_target_pairs={{0,2},{2,4},{4,6},{1,3},{3,5},{5,7},{8,10},{10,12},{12,14},{9,11},... | collective-permute-start | bytes 1572872 | tf_op jit(solution)/shard_map/ppermute | solution.py:17
  24.9 11.4 %collective-permute-start.3 = (f32[2,4,256,64]{2,3,1,0:T(8,128)}, f32[2,4,256,64]{2,3,1,0:T(8,128)}, u32[]{:S(2)}, u32[]{:S(2)}) collective-permute-start(f32[2,4,256,64]{2,3,1,0:T(8,128)} %get-tuple-element.337), channel_id=1, source_target_pairs={{2,0},{4,2},{6,4},{3,1},{5,3},{7,5},{10,8},{12,10},{14,12},{11,9},... | collective-permute-start | bytes 1572872 | tf_op jit(solution)/shard_map/ppermute | solution.py:18
  26.8 0.7 copy-start.4
  79.4 10.9 %collective-permute-start.4 = (f32[4,2,128,128]{3,2,0,1:T(8,128)S(1)}, f32[4,2,128,128]{3,2,0,1:T(8,128)S(1)}, u32[]{:S(2)}, u32[]{:S(2)}) collective-permute-start(f32[4,2,128,128]{3,2,0,1:T(8,128)S(1)} %pad_maximum_fusion.7), channel_id=1, source_target_pairs={{0,1},{2,3},{4,5},{6,7},{8,9},{10,11},{12,13},{14,15},{16,17},{18,... | collective-permute-start | bytes 1572872 | tf_op jit(solution)/shard_map/ppermute | solution.py:26
  112.1 4.5 copy-start.12
  144.9 12.6 %collective-permute-start.5 = (f32[4,2,128,128]{3,2,0,1:T(8,128)S(1)}, f32[4,2,128,128]{3,2,0,1:T(8,128)S(1)}, u32[]{:S(2)}, u32[]{:S(2)}) collective-permute-start(f32[4,2,128,128]{3,2,0,1:T(8,128)S(1)} %get-tuple-element.399), channel_id=1, source_target_pairs={{1,0},{3,2},{5,4},{7,6},{9,8},{11,10},{13,12},{15,14},{17,16},{19,... | collective-permute-start | bytes 1572872 | tf_op jit(solution)/shard_map/ppermute | solution.py:26
  146.2 0.9 copy-start.5
  232.5 2.3 copy-start.7
  232.5 2.3 copy-start.8
  232.6 2.3 copy-start.9
  232.6 2.3 copy-start.10
  285.6 11.5 %copy-start.15 = (s32[4]{0:T(128)S(1)}, s32[4]{0:T(128)}, u32[]{:S(2)}) copy-start(s32[4]{0:T(128)} %constant.360.clone.1) | copy-start | bytes 52
  286.9 15.6 %collective-permute-start.7 = (f32[2,4,64,384]{3,2,1,0:T(8,128)}, f32[2,4,64,384]{3,2,1,0:T(8,128)}, u32[]{:S(2)}, u32[]{:S(2)}) collective-permute-start(f32[2,4,64,384]{3,2,1,0:T(8,128)} %get-tuple-element.334), channel_id=1, source_target_pairs={{8,0},{16,8},{24,16},{9,1},{17,9},{25,17},{10,2},{18,10},{26,18},{... | collective-permute-start | bytes 2359304 | tf_op jit(solution)/shard_map/ppermute | solution.py:18
  288.2 17.1 %collective-permute-start.6 = (f32[2,4,64,384]{3,2,1,0:T(8,128)}, f32[2,4,64,384]{3,2,1,0:T(8,128)}, u32[]{:S(2)}, u32[]{:S(2)}) collective-permute-start(f32[2,4,64,384]{3,2,1,0:T(8,128)} %get-tuple-element.335), channel_id=1, source_target_pairs={{0,8},{8,16},{16,24},{1,9},{9,17},{17,25},{2,10},{10,18},{18,26},{... | collective-permute-start | bytes 2359304 | tf_op jit(solution)/shard_map/ppermute | solution.py:17
  298.4 3.4 copy-start.11
  311.3 118.6 %collective-permute-start.9 = (f32[2,4,384,64]{2,3,1,0:T(8,128)}, f32[2,4,384,64]{2,3,1,0:T(8,128)}, u32[]{:S(2)}, u32[]{:S(2)}) collective-permute-start(f32[2,4,384,64]{2,3,1,0:T(8,128)} %get-tuple-element.332), channel_id=1, source_target_pairs={{2,0},{4,2},{6,4},{3,1},{5,3},{7,5},{10,8},{12,10},{14,12},{11,9},... | collective-permute-start | bytes 2359304 | tf_op jit(solution)/shard_map/ppermute | solution.py:18
  357.7 75.6 %collective-permute-start.8 = (f32[2,4,384,64]{2,3,1,0:T(8,128)}, f32[2,4,384,64]{2,3,1,0:T(8,128)}, u32[]{:S(2)}, u32[]{:S(2)}) collective-permute-start(f32[2,4,384,64]{2,3,1,0:T(8,128)} %get-tuple-element.333), channel_id=1, source_target_pairs={{0,2},{2,4},{4,6},{1,3},{3,5},{5,7},{8,10},{10,12},{12,14},{9,11},... | collective-permute-start | bytes 2359304 | tf_op jit(solution)/shard_map/ppermute | solution.py:17
  433.0 2.9 copy-start
  437.6 4.2 copy-start.6
  453.4 1.0 copy-start.1
Sparse Core Ops, SparseCore 0:
  302.6 121.1 all-reduce.1
where the time goes:
time: 469 us; the launch traced here: 463 us
  local copies, waits for them, and re-layouts  111 us (24%)
  matrix products  97 us (21%)
  waiting for transfers between devices  89.4 us (19%)
  other arithmetic  43.4 us (9%)
  blocking collectives  42.4 us (9%)
  loops' own time  30.2 us (6%)
  starting transfers between devices  30.1 us (6%)
  between operations  18.6 us (4%)
    psum x1, waiting for transfers between devices, local(): totals = lax.psum((probe_part, error_part), ('sx', 'sy', 'depth'))  61.6 us
    dynamic_update_slice x8, local copies, waits for them, and re-layouts, add_one(): lax.dynamic_update_slice(accumulated, current + pieces[number], corner)  47.9 us
    psum x1, blocking collectives, local(): totals = lax.psum((probe_part, error_part), ('sx', 'sy', 'depth'))  42.4 us
    another operation x2, loops' own time, add_windows(): return lax.fori_loop(0, pieces.shape[0], add_one, gradient_ext)  29.9 us
    ppermute x4, starting transfers between devices, with_halo(): before = lax.ppermute(last, axis, up)  20.1 us
    gather x20, local copies, waits for them, and re-layouts  17.5 us
    ppermute x2, waiting for transfers between devices, from_behind(): lax.ppermute(value, axis, [(source, source + steps) for source in range(f...  16.8 us
    add x8, other arithmetic, add_one(): current + pieces[number]  16.5 us
  transfers between devices with their start and end apart: 11, of which 6 were waited for; matrix products, arithmetic and copies ran while one was open for 6% of the time, Pallas kernels for 0%

commit v1 on v0

v1 whole, which is shorter than its diff:
```python
import functools

import jax
import jax.numpy as jnp
import ml_dtypes
import numpy as np
from jax import lax
from jax.experimental import pallas as pl
from jax.experimental.pallas import tpu as pltpu
from jax.sharding import PartitionSpec as P

FRESNEL = 12.0
F32 = jnp.float32
BF16 = jnp.bfloat16


def split_table(table):
    high = table.astype(np.float32).astype(ml_dtypes.bfloat16)
    low = (table - high.astype(np.float64)).astype(np.float32).astype(ml_dtypes.bfloat16)
    return high, low


def build_tables(points):
    counter = np.arange(points)
    angles = (counter[:, None] * counter[None, :] % points) * (2.0 * np.pi / points)
    fourier = np.exp(-1j * angles) / np.sqrt(points)
    frequency = np.where(counter < points // 2, counter, counter - points) / points
    transfer = np.exp(-1j * FRESNEL * frequency * frequency)
    prop = (fourier * transfer[None, :]) @ fourier.conj()
    prop = 0.5 * (prop + prop.T)
    tables = []
    for matrix in (prop, fourier):
        re, im = matrix.real, matrix.imag
        right = np.block([[re, im], [-im, re]])
        left = np.block([[re, -im], [im, re]])
        tables.append(np.stack(split_table(right) + split_table(left)))
    return tables


def split(value):
    high = value.astype(BF16)
    low = (value - high.astype(F32)).astype(BF16)
    return high, low


def dot(a, b):
    return jnp.dot(a, b, preferred_element_type=F32)


def dot3(a, b):
    (a_high, a_low), (b_high, b_low) = a, b
    return dot(a_high, b_high) + (dot(a_high, b_low) + dot(a_low, b_high))


def apply_both(table_ref, fields, conj):
    n = fields[0].shape[0]
    first = 2 if conj else 0
    right = (table_ref[first], table_ref[first + 1])
    left = (table_ref[2 - first], table_ref[3 - first])
    mid = dot3(split(jnp.concatenate(fields, axis=0)), right)
    columns = [
        jnp.concatenate([mid[p * n : (p + 1) * n, :n], mid[p * n : (p + 1) * n, n:]], axis=0)
        for p in range(len(fields))
    ]
    out = dot3(left, split(jnp.concatenate(columns, axis=1)))
    return [
        jnp.concatenate([out[:n, p * n : (p + 1) * n], out[n:, p * n : (p + 1) * n]], axis=1)
        for p in range(len(fields))
    ]


def times(a, b):
    n = a.shape[-1] // 2
    ar, ai, br, bi = a[:, :n], a[:, n:], b[:, :n], b[:, n:]
    return jnp.concatenate([ar * br - ai * bi, ar * bi + ai * br], axis=1)


def conj_times(a, b):
    n = a.shape[-1] // 2
    ar, ai, br, bi = a[:, :n], a[:, n:], b[:, :n], b[:, n:]
    return jnp.concatenate([ar * br + ai * bi, ar * bi - ai * br], axis=1)


def groups_of(positions):
    size = 2 if positions % 2 == 0 else 1
    return [list(range(s, s + size)) for s in range(0, positions, size)]


def forward(prop_ref, factor_ref, incident_ref, wave_ref):
    positions, slabs = factor_ref.shape[:2]

    @pl.loop(0, slabs)
    def _(k):
        for group in groups_of(positions):
            waves = [wave_ref[p] for p in group]
            for p, wave in zip(group, waves):
                incident_ref[p, k] = wave
            waves = [times(wave, factor_ref[p, k]) for p, wave in zip(group, waves)]
            for p, wave in zip(group, apply_both(prop_ref, waves, False)):
                wave_ref[p] = wave


def backward(prop_ref, factor_ref, incident_ref, wave_ref, emit):
    positions, slabs = factor_ref.shape[:2]

    @pl.loop(0, slabs)
    def _(step):
        k = slabs - 1 - step
        for group in groups_of(positions):
            waves = apply_both(prop_ref, [wave_ref[p] for p in group], True)
            for p, wave in zip(group, waves):
                emit(p, k, conj_times(incident_ref[p, k], wave))
                wave_ref[p] = conj_times(factor_ref[p, k], wave)


def cut_kernel(off_ref, own_ref, left_ref, right_ref, up_ref, down_ref, ul_ref, ur_ref, dl_ref,
               dr_ref, factor_ref, ext):
    positions, slabs, n, _ = factor_ref.shape
    rows, cols = own_ref.shape[2:]
    b = n // 2
    for k in range(slabs):
        for part in range(2):
            ext[part, k, b : b + rows, n : n + cols] = own_ref[part, k]
            ext[part, k, :b, n : n + cols] = up_ref[part, k]
            ext[part, k, b + rows : n + rows, n : n + cols] = down_ref[part, k]
            for left, right, at, size in (
                (ul_ref, ur_ref, 0, b), (left_ref, right_ref, b, rows), (dl_ref, dr_ref, b + rows, b)
            ):
                x, y = left[k], right[k]
                if part == 0:
                    x = pltpu.roll(x, b, 1)
                else:
                    y = pltpu.roll(y, b, 1)
                ext[part, k, at : at + size, :n] = x
                ext[part, k, at : at + size, n + cols :] = y
    for p in range(positions):
        down = lax.rem(off_ref[p, 0] + b, 8)
        row = pl.multiple_of(off_ref[p, 0] + b - down, 8)
        col = off_ref[p, 1] + n
        block = jnp.minimum(col // n, (cols + n) // n - 1)
        start = pl.multiple_of(block * n, n)
        shift = lax.rem(4 * n - (col - start), 2 * n)
        for k in range(slabs):
            parts = []
            for part in range(2):
                wide = ext[part, k, pl.ds(row, n + 8), pl.ds(start, 2 * n)]
                wide = pltpu.roll(wide, shift, 1)[:, :n]
                parts.append(pltpu.roll(wide, lax.rem(n + 8 - down, n + 8), 0)[:n])
            factor_ref[p, k] = jnp.concatenate([1.0 + parts[0], parts[1]], axis=1)


def first_kernel(wave_in, factor_ref, prop_ref, wave_out, incident):
    wave_out[...] = wave_in[...]
    forward(prop_ref, factor_ref, incident, wave_out)


def middle_kernel(shift_ref, wave_in, factor_ref, patterns_ref, prop_ref, fourier_ref,
                  grad_exit, grad_start, incident, error_ref):
    positions, _, n, _ = factor_ref.shape
    grad_start[...] = wave_in[...]
    forward(prop_ref, factor_ref, incident, grad_start)
    error = jnp.zeros((8, n), F32)
    for group in groups_of(positions):
        fars = apply_both(fourier_ref, [grad_start[p] for p in group], False)
        grads = []
        for p, far in zip(group, fars):
            measured = patterns_ref[p]
            measured = pltpu.roll(measured, lax.rem(2 * n - shift_ref[p, 0], n), 0)
            measured = pltpu.roll(measured, lax.rem(2 * n - shift_ref[p, 1], n), 1)
            fr, fi = far[:, :n], far[:, n:]
            residual = fr * fr + fi * fi - measured
            error += jnp.sum((residual * residual).reshape(n // 8, 8, n), axis=0)
            residual = 2.0 * residual
            grads.append(jnp.concatenate([residual * fr, residual * fi], axis=1))
        for p, grad in zip(group, apply_both(fourier_ref, grads, True)):
            grad_exit[p] = grad
    error_ref[...] = error * 0.5
    grad_start[...] = grad_exit[...]
    backward(prop_ref, factor_ref, incident, grad_start, lambda p, k, piece: None)


def last_kernel(off_ref, wave_in, factor_ref, incident_ref, prop_ref, grad_start, center, up, down,
                left_ref, right_ref, ul_ref, ur_ref, dl_ref, dr_ref, ext):
    positions, slabs, n, _ = factor_ref.shape
    rows, cols = center.shape[2:]
    b = n // 2
    ext[...] = jnp.zeros_like(ext)
    grad_start[...] = wave_in[...]

    def emit(p, k, piece):
        down = lax.rem(off_ref[p, 0] + b, 8)
        row = pl.multiple_of(off_ref[p, 0] + b - down, 8)
        col = off_ref[p, 1] + n
        block = jnp.minimum(col // n, (cols + n) // n - 1)
        start = pl.multiple_of(block * n, n)
        shift = lax.rem(col - start, 2 * n)
        for part in range(2):
            value = piece[:, part * n : (part + 1) * n]
            value = jnp.concatenate([value, jnp.zeros((8, n), F32)], axis=0)
            value = pltpu.roll(value, down, 0)
            wide = pltpu.roll(jnp.concatenate([value, jnp.zeros_like(value)], axis=1), shift, 1)
            ext[part, k, pl.ds(row, n + 8), pl.ds(start, 2 * n)] += wide

    backward(prop_ref, factor_ref, incident_ref, grad_start, emit)
    lane = lax.broadcasted_iota(jnp.int32, (1, n), 1)
    for k in range(slabs):
        for part in range(2):
            center[part, k] = ext[part, k, b : b + rows, n : n + cols]
            up[part, k] = ext[part, k, :b, n : n + cols]
            down[part, k] = ext[part, k, b + rows : n + rows, n : n + cols]
        for left, right, at, size in (
            (ul_ref, ur_ref, 0, b), (left_ref, right_ref, b, rows), (dl_ref, dr_ref, b + rows, b)
        ):
            re, im = (ext[part, k, at : at + size, :n] for part in range(2))
            left[k] = jnp.where(lane < b, pltpu.roll(re, b, 1), im)
            re, im = (ext[part, k, at : at + size, n + cols :] for part in range(2))
            right[k] = jnp.where(lane < b, re, pltpu.roll(im, b, 1))


def fold_kernel(center, up, down, left_ref, right_ref, ul_ref, ur_ref, dl_ref, dr_ref, out):
    slabs, rows, cols = center.shape[1:]
    b = up.shape[2]
    n = 2 * b
    lane = lax.broadcasted_iota(jnp.int32, (1, n), 1)
    for k in range(slabs):
        for part in range(2):
            out[part, k] = center[part, k]
            out[part, k, :b] += up[part, k]
            out[part, k, rows - b :] += down[part, k]
            for left, right, at, size in (
                (left_ref, right_ref, 0, rows), (ul_ref, ur_ref, 0, b), (dl_ref, dr_ref, rows - b, b)
            ):
                x, y = left[k], right[k]
                if part == 1:
                    x = pltpu.roll(x, b, 1)
                else:
                    y = pltpu.roll(y, b, 1)
                out[part, k, at : at + size, :n] += jnp.where(lane < b, x, 0.0)
                out[part, k, at : at + size, cols - n :] += jnp.where(lane < b, 0.0, y)


VMEM = pl.BlockSpec(memory_space=pltpu.VMEM)
SMEM = pl.BlockSpec(memory_space=pltpu.SMEM)


def call(kernel, args, outs, smem=0, scratch=(), flops=0):
    return pl.pallas_call(
        kernel,
        out_shape=[jax.ShapeDtypeStruct(shape, F32) for shape in outs],
        in_specs=[SMEM] * smem + [VMEM] * (len(args) - smem),
        out_specs=[VMEM] * len(outs),
        scratch_shapes=[pltpu.VMEM(shape, F32) for shape in scratch],
        compiler_params=pltpu.CompilerParams(vmem_limit_bytes=48 * 1024 * 1024),
        cost_estimate=pl.CostEstimate(flops=flops, bytes_accessed=0, transcendentals=0),
    )(*args)


def shifted(value, down, right):
    rows, cols = lax.axis_size("sx"), lax.axis_size("sy")
    if right == 0:
        return lax.ppermute(value, "sx", [(i, i + down) for i in range(rows) if 0 <= i + down < rows])
    if down == 0:
        return lax.ppermute(value, "sy", [(i, i + right) for i in range(cols) if 0 <= i + right < cols])
    pairs = [
        (i * cols + j, (i + down) * cols + j + right)
        for i in range(rows)
        for j in range(cols)
        if 0 <= i + down < rows and 0 <= j + right < cols
    ]
    return lax.ppermute(value, ("sx", "sy"), pairs)


def local(probe_wave, transmission, scan_offsets, pattern_shifts, patterns):
    n = probe_wave.shape[-1]
    b = n // 2
    _, slabs, rows, cols = transmission.shape
    prop_table, fourier_table = (jnp.asarray(t) for t in build_tables(n))
    offsets = scan_offsets.reshape(-1, 2)
    shifts = pattern_shifts.reshape(-1, 2)
    measured = patterns.reshape(-1, n, n)
    positions = offsets.shape[0]
    depth = lax.axis_size("depth")
    index = lax.axis_index("depth")

    first = jnp.concatenate([transmission[0, :, :, :b], transmission[1, :, :, :b]], axis=-1)
    last = jnp.concatenate([transmission[0, :, :, cols - b :], transmission[1, :, :, cols - b :]], axis=-1)
    rims = [
        shifted(last, 0, 1),
        shifted(first, 0, -1),
        shifted(transmission[:, :, rows - b :], 1, 0),
        shifted(transmission[:, :, :b], -1, 0),
        shifted(last[:, rows - b :], 1, 1),
        shifted(first[:, rows - b :], 1, -1),
        shifted(last[:, :b], -1, 1),
        shifted(first[:, :b], -1, -1),
    ]
    wave_shape = (positions, n, 2 * n)
    store_shape = (positions, slabs, n, 2 * n)
    ext_shape = (2, slabs, rows + n + 8, cols + 2 * n)
    (factor,) = call(cut_kernel, [offsets, transmission, *rims], [store_shape], smem=1, scratch=[ext_shape])

    probe = jnp.broadcast_to(jnp.concatenate([probe_wave[0], probe_wave[1]], axis=-1)[None], wave_shape)
    forward_pairs = [(i, i + 1) for i in range(depth - 1)]
    backward_pairs = [(i + 1, i) for i in range(depth - 1)]
    entering = probe
    for _ in range(depth - 1):
        leaving, _ = call(first_kernel, [entering, factor, prop_table], [wave_shape, store_shape])
        incoming = lax.ppermute(leaving, "depth", forward_pairs)
        entering = jnp.where(index == 0, probe, incoming)
    grad_exit, grad_start, incident, error = call(
        middle_kernel, [shifts, entering, factor, measured, prop_table, fourier_table],
        [wave_shape, wave_shape, store_shape, (8, n)], smem=1,
    )
    for round_number in range(depth - 1):
        incoming = lax.ppermute(grad_start, "depth", backward_pairs)
        entering = jnp.where(index == depth - 1, grad_exit, incoming)
        grad_start, center, up, down, left, right, ul, ur, dl, dr = call(
            last_kernel, [offsets, entering, factor, incident, prop_table],
            [wave_shape, transmission.shape, (2, slabs, b, cols), (2, slabs, b, cols),
             (slabs, rows, n), (slabs, rows, n)] + [(slabs, b, n)] * 4,
            smem=1, scratch=[ext_shape],
        )
    probe_part = jnp.where(index == 0, jnp.sum(grad_start, axis=0), 0.0)
    error_part = jnp.where(index == depth - 1, error, 0.0)
    totals = lax.psum(jnp.concatenate([probe_part, jnp.concatenate([error_part, error_part * 0.0], axis=-1)], axis=0), ("sx", "sy", "depth"))
    (transmission_grad,) = call(
        fold_kernel,
        [center, shifted(down, 1, 0), shifted(up, -1, 0), shifted(right, 0, 1), shifted(left, 0, -1),
         shifted(dr, 1, 1), shifted(dl, 1, -1), shifted(ur, -1, 1), shifted(ul, -1, -1)],
        [transmission.shape],
    )
    all_positions = positions * lax.axis_size("sx") * lax.axis_size("sy")
    probe_grad = jnp.stack([totals[:n, :n], totals[:n, n:]]) / all_positions
    mean_error = jnp.sum(totals[n:]) / (all_positions * n * n)
    return (transmission_grad, probe_grad, mean_error)


def solution(mesh):
    in_specs = (
        P(),
        P(None, "depth", "sx", "sy"),
        P("sx", "sy", None, None),
        P("sx", "sy", None, None),
        P("sx", "sy", None, None, None),
    )
    out_specs = (P(None, "depth", "sx", "sy"), P(), P())
    return jax.shard_map(local, mesh=mesh, in_specs=in_specs, out_specs=out_specs, check_vma=False)
```

time: 469 us -> 260 us (0.55)
  matrix products: 97 us -> 0 us
  local copies, waits for them, and re-layouts: 111 us -> 16.7 us
  waiting for transfers between devices: 89.4 us -> 144 us
  blocking collectives: 42.4 us -> 0 us
  other arithmetic: 43.4 us -> 7.14 us
  loops' own time: 30.2 us -> 0 us
  Pallas kernels: 0 us -> 27.6 us
  starting transfers between devices: 30.1 us -> 44.4 us
    dot_general x152 -> x0, matrix products: 97 us -> none  [the longest x18 14.6 us: right_apply(): jnp.einsum('nij,jk->nik', field_imag, matrix_imag, precision=PRECISE)]
    psum x1, waiting for transfers between devices: 61.6 us -> 111 us  [local(): lax.psum(jnp.concatenate([probe_part, jnp.concatenate([error_part, error_...]
    dynamic_update_slice x8 -> x0, local copies, waits for them, and re-layouts: 47.9 us -> none  [add_one(): lax.dynamic_update_slice(accumulated, current + pieces[number], corner)]
    psum x1 -> x0, blocking collectives: 42.4 us -> none  [local(): totals = lax.psum((probe_part, error_part), ('sx', 'sy', 'depth'))]
    another operation x3 -> x0, loops' own time: 30.2 us -> none  [the longest x2 29.9 us: add_windows(): return lax.fori_loop(0, pieces.shape[0], add_one, gradient_ext)]
    pallas_call x0 -> x5, Pallas kernels: none -> 27.6 us  [call(): pl.pallas_call(kernel, out_shape=[jax.ShapeDtypeStruct(shape, F32) for sh...]
    add x15 -> x0, other arithmetic: 17.6 us -> none  [the longest x8 16.5 us: add_one(): current + pieces[number]]
    gather x20 -> x0, local copies, waits for them, and re-layouts: 17.5 us -> none
  transfers between devices with their start and end apart: 11 -> 19, of which waited for: 6 -> 6; matrix products, arithmetic and copies ran while one was open for 6% -> 3% of each run, Pallas kernels for 0% -> 0%
where the time goes in v1:
time: 260 us; the launch traced here: 256 us
  waiting for transfers between devices  144 us (55%)
  starting transfers between devices  44.4 us (17%)
  Pallas kernels  27.6 us (11%)
  local copies, waits for them, and re-layouts  16.7 us (6%)
  between operations  16.2 us (6%)
  other arithmetic  7.14 us (3%)
    psum x1, waiting for transfers between devices, local(): lax.psum(jnp.concatenate([probe_part, jnp.concatenate([error_part, error_...  111 us
    pallas_call x5, Pallas kernels, call(): pl.pallas_call(kernel, out_shape=[jax.ShapeDtypeStruct(shape, F32) for sh...  27.6 us
    ppermute x4, starting transfers between devices, shifted(): lax.ppermute(value, 'sx', [(i, i + down) for i in range(rows) if 0 <= i +...  15.7 us
    ppermute x1, waiting for transfers between devices, local(): incoming = lax.ppermute(grad_start, 'depth', backward_pairs)  14.8 us
    ppermute x8, starting transfers between devices, shifted(): return lax.ppermute(value, ('sx', 'sy'), pairs)  12.4 us
    ppermute x1, waiting for transfers between devices, local(): incoming = lax.ppermute(leaving, 'depth', forward_pairs)  11.7 us
    unnamed x44, local copies, waits for them, and re-layouts  11.3 us
    ppermute x4, starting transfers between devices, shifted(): lax.ppermute(value, 'sy', [(i, i + right) for i in range(cols) if 0 <= i...  10.7 us
  transfers between devices with their start and end apart: 19, of which 6 were waited for; matrix products, arithmetic and copies ran while one was open for 3% of the time, Pallas kernels for 0%

profile of v1, /device:TPU:0, one launch (start us, length us, event | category | flops | bytes accessed | tf_op | source)
XLA Modules:
  0.0 255.9 jit_solution(7139790858170818518)
XLA Ops:
  7.2 1.5 slice_bitcast_fusion.1
  8.8 4.4 %collective-permute-start.4 = (f32[4,64,128]{2,1,0:T(8,128)S(1)}, f32[4,64,128]{2,1,0:T(8,128)S(1)}, u32[]{:S(2)}, u32[]{:S(2)}) collective-permute-start(f32[4,64,128]{2,1,0:T(8,128)S(1)} %get-tuple-element.44), channel_id=1, source_target_pairs={{0,10},{2,12},{4,14},{8,18},{10,20},{12,22},{16,26},{18,28},{20,30... | collective-permute-start | bytes 393224 | tf_op jit(solution)/shard_map/ppermute | solution.py:270
  15.5 1.1 fusion.4
  16.6 7.8 %collective-permute-start.2 = (f32[2,4,64,256]{3,2,1,0:T(8,128)}, f32[2,4,64,256]{3,2,1,0:T(8,128)S(1)}, u32[]{:S(2)}, u32[]{:S(2)}) collective-permute-start(f32[2,4,64,256]{3,2,1,0:T(8,128)} %get-tuple-element.36), channel_id=1, source_target_pairs={{0,8},{8,16},{16,24},{1,9},{9,17},{17,25},{2,10},{10,18},{18,26},{... | collective-permute-start | bytes 1572872 | tf_op jit(solution)/shard_map/ppermute | solution.py:261
  24.3 1.3 collective-permute-start.3
  26.6 1.3 collective-permute-start.7
  28.6 1.3 collective-permute-start.1
  30.5 4.5 %collective-permute-start = (f32[4,128,128]{2,1,0:T(8,128)S(1)}, f32[4,128,128]{2,1,0:T(8,128)S(1)}, u32[]{:S(2)}, u32[]{:S(2)}) collective-permute-start(f32[4,128,128]{2,1,0:T(8,128)S(1)} %pad_maximum_fusion), channel_id=1, source_target_pairs={{0,2},{2,4},{4,6},{1,3},{3,5},{5,7},{8,10},{10,12},{12,14},{9,11},... | collective-permute-start | bytes 786440 | tf_op jit(solution)/shard_map/ppermute | solution.py:263
  36.5 2.2 collective-permute-done.1.right_ref
  38.7 2.2 collective-permute-done.left_ref
  49.0 2.3 shard_map.94.factor_ref
  51.4 1.1 broadcast_in_dim.14.wave_in
  52.6 4.5 %shard_map.95 = (f32[4,128,256]{2,1,0:T(8,128)}, f32[4,4,128,256]{3,2,1,0:T(8,128)}) custom-call(f32[4,128,256]{2,1,0:T(8,128)S(1)} %broadcast_in_dim.14.wave_in, f32[4,4,128,256]{3,2,1,0:T(8,128)S(1)} %shard_map.94.factor_ref, bf16[4,256,256]{2,1,0:T(8,128)(2,1)S(1)} %copy-done.2), custom_call_target="tpu_custom_call" | custom-call | tf_op jit(solution)/shard_map/pallas_call | solution.py:247
  57.0 4.2 %collective-permute-start.8 = (f32[4,128,256]{2,1,0:T(8,128)}, f32[4,128,256]{2,1,0:T(8,128)}, u32[]{:S(2)}, u32[]{:S(2)}) collective-permute-start(f32[4,128,256]{2,1,0:T(8,128)} %get-tuple-element.18), channel_id=1, source_target_pairs={{0,1},{2,3},{4,5},{6,7},{8,9},{10,11},{12,13},{14,15},{16,17},{18,... | collective-permute-start | bytes 1572872 | tf_op jit(solution)/shard_map/ppermute | solution.py:308
  61.3 11.7 %collective-permute-done.8 = f32[4,128,256]{2,1,0:T(8,128)} collective-permute-done((f32[4,128,256]{2,1,0:T(8,128)}, f32[4,128,256]{2,1,0:T(8,128)}, u32[]{:S(2)}, u32[]{:S(2)}) %collective-permute-start.8) | collective-permute-done | bytes 524320 | tf_op jit(solution)/shard_map/ppermute | solution.py:308
  74.0 10.9 %shard_map.96 = (f32[4,128,256]{2,1,0:T(8,128)S(1)}, f32[4,128,256]{2,1,0:T(8,128)S(1)}, f32[4,4,128,256]{3,2,1,0:T(8,128)S(1)}, f32[8,128]{1,0:T(8,128)S(1)}) custom-call(s32[4,2]{1,0:T(4,128)S(1)} %copy.11.shift_ref, f32[4,128,256]{2,1,0:T(8,128)S(1)} %broadcast_select_fusion.wave_in, f32[4,4,128,256]{3,2,1,0:T(8,128)} %copy-done, ...), custom_call_target="tpu_custom_call" | custom-call | tf_op jit(solution)/shard_map/pallas_call | solution.py:247
  85.0 1.3 copy-done.4
  86.3 1.3 collective-permute-start.9
  87.6 14.8 %collective-permute-done.9 = f32[4,128,256]{2,1,0:T(8,128)S(1)} collective-permute-done((f32[4,128,256]{2,1,0:T(8,128)S(1)}, f32[4,128,256]{2,1,0:T(8,128)S(1)}, u32[]{:S(2)}, u32[]{:S(2)}) %collective-permute-start.9) | collective-permute-done | bytes 524320 | tf_op jit(solution)/shard_map/ppermute | solution.py:315
  102.4 8.5 %shard_map.97 = (f32[4,128,256]{2,1,0:T(8,128)S(1)}, f32[2,4,128,256]{3,2,1,0:T(8,128)S(1)}, f32[2,4,64,256]{3,2,1,0:T(8,128)}, f32[2,4,64,256]{3,2,1,0:T(8,128)...) custom-call(s32[4,2]{1,0:T(4,128)S(1)} %copy.12.off_ref, ...), custom_call_target="tpu_custom_call" | custom-call | tf_op jit(solution)/shard_map/pallas_call | solution.py:247
  111.0 2.6 %collective-permute-start.14 = (f32[4,64,128]{2,1,0:T(8,128)}, f32[4,64,128]{2,1,0:T(8,128)S(1)}, u32[]{:S(2)}, u32[]{:S(2)}) collective-permute-start(f32[4,64,128]{2,1,0:T(8,128)} %get-tuple-element.27), channel_id=1, source_target_pairs={{0,10},{2,12},{4,14},{8,18},{10,20},{12,22},{16,26},{18,28},{20,30... | collective-permute-start | bytes 393224 | tf_op jit(solution)/shard_map/ppermute | solution.py:270
  115.0 5.4 %collective-permute-start.10 = (f32[2,4,64,256]{3,2,1,0:T(8,128)}, f32[2,4,64,256]{3,2,1,0:T(8,128)S(1)}, u32[]{:S(2)}, u32[]{:S(2)}) collective-permute-start(f32[2,4,64,256]{3,2,1,0:T(8,128)} %get-tuple-element.23), channel_id=1, source_target_pairs={{0,8},{8,16},{16,24},{1,9},{9,17},{17,25},{2,10},{10,18},{18,26},{... | collective-permute-start | bytes 1572872 | tf_op jit(solution)/shard_map/ppermute | solution.py:261
  120.4 1.3 collective-permute-start.11
  121.7 3.6 %collective-permute-start.12 = (f32[4,128,128]{2,1,0:T(8,128)}, f32[4,128,128]{2,1,0:T(8,128)S(1)}, u32[]{:S(2)}, u32[]{:S(2)}) collective-permute-start(f32[4,128,128]{2,1,0:T(8,128)} %get-tuple-element.25), channel_id=1, source_target_pairs={{0,2},{2,4},{4,6},{1,3},{3,5},{5,7},{8,10},{10,12},{12,14},{9,11},... | collective-permute-start | bytes 786440 | tf_op jit(solution)/shard_map/ppermute | solution.py:263
  125.3 1.3 collective-permute-start.13
  127.3 111.5 %all-reduce.2.cloned.1.call-done = f32[136,256]{1,0:T(8,128)} async-done(((f32[136,256]{1,0:T(8,128)}), f32[136,256]{1,0:T(8,128)}) %all-reduce.2.cloned.1.call-update) | async-done | bytes 139280 | tf_op jit(solution)/shard_map/psum | solution.py:325
  238.8 1.5 slice_bitcast_fusion.5
  240.3 1.3 collective-permute-start.17
  241.6 1.3 slice_reduce_fusion
  243.5 1.5 maximum_multiply_fusion
  245.1 1.5 collective-permute-done.17.dr_ref
  246.6 1.4 shard_map.98
  (76 shorter events, 17.4 us)
Async XLA Ops:
  7.2 8.3 %copy-start.1 = (f32[2,4,128,256]{3,2,1,0:T(8,128)S(1)}, f32[2,4,128,256]{3,2,1,0:T(8,128)}, u32[]{:S(2)}) copy-start(f32[2,4,128,256]{3,2,1,0:T(8,128)} %own_ref.1) | copy-start | bytes 3145732
  7.2 231.6 %all-reduce.2.cloned.1.call-start = ((), (), s32[]{:S(2)}) async-start(), calls=%async_computation | async-start | bytes 278528 | tf_op jit(solution)/shard_map/psum | solution.py:325
  8.8 17.8 %collective-permute-start.4 = (f32[4,64,128]{2,1,0:T(8,128)S(1)}, f32[4,64,128]{2,1,0:T(8,128)S(1)}, u32[]{:S(2)}, u32[]{:S(2)}) collective-permute-start(f32[4,64,128]{2,1,0:T(8,128)S(1)} %get-tuple-element.44), channel_id=1, source_target_pairs={{0,10},{2,12},{4,14},{8,18},{10,20},{12,22},{16,26},{18,28},{20,30... | collective-permute-start | bytes 393224 | tf_op jit(solution)/shard_map/ppermute | solution.py:270
  13.2 21.9 %copy-start.19 = (f32[2,128,128]{2,1,0:T(8,128)S(1)}, f32[2,128,128]{2,1,0:T(8,128)}, u32[]{:S(2)}) copy-start(f32[2,128,128]{2,1,0:T(8,128)} %param.7) | copy-start | bytes 393220
  14.0 21.1 %copy-start.20 = (s32[1,1,4,2]{2,3,1,0:T(2,128)S(1)}, s32[1,1,4,2]{2,3,1,0:T(2,128)}, u32[]{:S(2)}) copy-start(s32[1,1,4,2]{2,3,1,0:T(2,128)} %param.9) | copy-start | bytes 100
  14.0 13.9 %collective-permute-start.5 = (f32[4,64,128]{2,1,0:T(8,128)S(1)}, f32[4,64,128]{2,1,0:T(8,128)S(1)}, u32[]{:S(2)}, u32[]{:S(2)}) collective-permute-start(f32[4,64,128]{2,1,0:T(8,128)S(1)} %get-tuple-element.42), channel_id=1, source_target_pairs={{2,8},{4,10},{6,12},{10,16},{12,18},{14,20},{18,24},{20,26},{22,28... | collective-permute-start | bytes 393224 | tf_op jit(solution)/shard_map/ppermute | solution.py:270
  14.8 15.1 %collective-permute-start.6 = (f32[4,64,128]{2,1,0:T(8,128)S(1)}, f32[4,64,128]{2,1,0:T(8,128)S(1)}, u32[]{:S(2)}, u32[]{:S(2)}) collective-permute-start(f32[4,64,128]{2,1,0:T(8,128)S(1)} %get-tuple-element.43), channel_id=1, source_target_pairs={{8,2},{10,4},{12,6},{16,10},{18,12},{20,14},{24,18},{26,20},{28,22... | collective-permute-start | bytes 393224 | tf_op jit(solution)/shard_map/ppermute | solution.py:270
  16.6 25.1 %collective-permute-start.2 = (f32[2,4,64,256]{3,2,1,0:T(8,128)}, f32[2,4,64,256]{3,2,1,0:T(8,128)S(1)}, u32[]{:S(2)}, u32[]{:S(2)}) collective-permute-start(f32[2,4,64,256]{3,2,1,0:T(8,128)} %get-tuple-element.36), channel_id=1, source_target_pairs={{0,8},{8,16},{16,24},{1,9},{9,17},{17,25},{2,10},{10,18},{18,26},{... | collective-permute-start | bytes 1572872 | tf_op jit(solution)/shard_map/ppermute | solution.py:261
  24.3 18.2 %collective-permute-start.3 = (f32[2,4,64,256]{3,2,1,0:T(8,128)}, f32[2,4,64,256]{3,2,1,0:T(8,128)S(1)}, u32[]{:S(2)}, u32[]{:S(2)}) collective-permute-start(f32[2,4,64,256]{3,2,1,0:T(8,128)} %get-tuple-element.35), channel_id=1, source_target_pairs={{8,0},{16,8},{24,16},{9,1},{17,9},{25,17},{10,2},{18,10},{26,18},{... | collective-permute-start | bytes 1572872 | tf_op jit(solution)/shard_map/ppermute | solution.py:261
  26.6 9.3 %collective-permute-start.7 = (f32[4,64,128]{2,1,0:T(8,128)}, f32[4,64,128]{2,1,0:T(8,128)S(1)}, u32[]{:S(2)}, u32[]{:S(2)}) collective-permute-start(f32[4,64,128]{2,1,0:T(8,128)} %get-tuple-element.41), channel_id=1, source_target_pairs={{10,0},{12,2},{14,4},{18,8},{20,10},{22,12},{26,16},{28,18},{30,20... | collective-permute-start | bytes 393224 | tf_op jit(solution)/shard_map/ppermute | solution.py:270
  28.6 10.1 %collective-permute-start.1 = (f32[4,128,128]{2,1,0:T(8,128)}, f32[4,128,128]{2,1,0:T(8,128)S(1)}, u32[]{:S(2)}, u32[]{:S(2)}) collective-permute-start(f32[4,128,128]{2,1,0:T(8,128)} %pad_maximum_fusion.1), channel_id=1, source_target_pairs={{2,0},{4,2},{6,4},{3,1},{5,3},{7,5},{10,8},{12,10},{14,12},{11,9},... | collective-permute-start | bytes 786440 | tf_op jit(solution)/shard_map/ppermute | solution.py:263
  30.5 10.4 %collective-permute-start = (f32[4,128,128]{2,1,0:T(8,128)S(1)}, f32[4,128,128]{2,1,0:T(8,128)S(1)}, u32[]{:S(2)}, u32[]{:S(2)}) collective-permute-start(f32[4,128,128]{2,1,0:T(8,128)S(1)} %pad_maximum_fusion), channel_id=1, source_target_pairs={{0,2},{2,4},{4,6},{1,3},{3,5},{5,7},{8,10},{10,12},{12,14},{9,11},... | collective-permute-start | bytes 786440 | tf_op jit(solution)/shard_map/ppermute | solution.py:263
  35.9 16.6 %copy-start.2 = (bf16[4,256,256]{2,1,0:T(8,128)(2,1)S(1)}, bf16[4,256,256]{2,1,0:T(8,128)(2,1)}, u32[]{:S(2)}) copy-start(bf16[4,256,256]{2,1,0:T(8,128)(2,1)} %constant.21.clone.prop_ref) | copy-start | bytes 1572868
  43.3 1.0 copy-start.7
  44.3 1.0 copy-start.9
  45.4 0.9 copy-start.12
  51.3 22.6 %copy-start = (f32[4,4,128,256]{3,2,1,0:T(8,128)}, f32[4,4,128,256]{3,2,1,0:T(8,128)S(1)}, u32[]{:S(2)}) copy-start(f32[4,4,128,256]{3,2,1,0:T(8,128)S(1)} %shard_map.94.factor_ref) | copy-start | bytes 6291460
  51.4 9.9 %copy-start.21 = (s32[1,1,4,2]{2,3,1,0:T(2,128)S(1)}, s32[1,1,4,2]{2,3,1,0:T(2,128)}, u32[]{:S(2)}) copy-start(s32[1,1,4,2]{2,3,1,0:T(2,128)} %param.10) | copy-start | bytes 100
  52.5 21.5 %copy-start.3 = (bf16[4,256,256]{2,1,0:T(8,128)(2,1)S(1)}, bf16[4,256,256]{2,1,0:T(8,128)(2,1)}, u32[]{:S(2)}) copy-start(bf16[4,256,256]{2,1,0:T(8,128)(2,1)} %constant.21.clone.prop_ref) | copy-start | bytes 1572868
  52.5 21.5 %copy-start.5 = (bf16[4,256,256]{2,1,0:T(8,128)(2,1)S(1)}, bf16[4,256,256]{2,1,0:T(8,128)(2,1)}, u32[]{:S(2)}) copy-start(bf16[4,256,256]{2,1,0:T(8,128)(2,1)} %constant.22.clone.fourier_ref) | copy-start | bytes 1572868
  52.5 21.5 %copy-start.10 = (f32[1,1,4,128,128]{4,3,2,1,0:T(8,128)S(1)}, f32[1,1,4,128,128]{4,3,2,1,0:T(8,128)}, u32[]{:S(2)}) copy-start(f32[1,1,4,128,128]{4,3,2,1,0:T(8,128)} %param.11) | copy-start | bytes 786436
  57.0 16.0 %collective-permute-start.8 = (f32[4,128,256]{2,1,0:T(8,128)}, f32[4,128,256]{2,1,0:T(8,128)}, u32[]{:S(2)}, u32[]{:S(2)}) collective-permute-start(f32[4,128,256]{2,1,0:T(8,128)} %get-tuple-element.18), channel_id=1, source_target_pairs={{0,1},{2,3},{4,5},{6,7},{8,9},{10,11},{12,13},{14,15},{16,17},{18,... | collective-permute-start | bytes 1572872 | tf_op jit(solution)/shard_map/ppermute | solution.py:308
  85.0 1.3 copy-start.4
  86.3 16.1 %collective-permute-start.9 = (f32[4,128,256]{2,1,0:T(8,128)S(1)}, f32[4,128,256]{2,1,0:T(8,128)S(1)}, u32[]{:S(2)}, u32[]{:S(2)}) collective-permute-start(f32[4,128,256]{2,1,0:T(8,128)S(1)} %get-tuple-element.20), channel_id=1, source_target_pairs={{1,0},{3,2},{5,4},{7,6},{9,8},{11,10},{13,12},{15,14},{17,16},{19,... | collective-permute-start | bytes 1572872 | tf_op jit(solution)/shard_map/ppermute | solution.py:315
  111.0 14.3 %collective-permute-start.14 = (f32[4,64,128]{2,1,0:T(8,128)}, f32[4,64,128]{2,1,0:T(8,128)S(1)}, u32[]{:S(2)}, u32[]{:S(2)}) collective-permute-start(f32[4,64,128]{2,1,0:T(8,128)} %get-tuple-element.27), channel_id=1, source_target_pairs={{0,10},{2,12},{4,14},{8,18},{10,20},{12,22},{16,26},{18,28},{20,30... | collective-permute-start | bytes 393224 | tf_op jit(solution)/shard_map/ppermute | solution.py:270
  113.6 13.0 %collective-permute-start.15 = (f32[4,64,128]{2,1,0:T(8,128)S(1)}, f32[4,64,128]{2,1,0:T(8,128)S(1)}, u32[]{:S(2)}, u32[]{:S(2)}) collective-permute-start(f32[4,64,128]{2,1,0:T(8,128)S(1)} %get-tuple-element.28), channel_id=1, source_target_pairs={{2,8},{4,10},{6,12},{10,16},{12,18},{14,20},{18,24},{20,26},{22,28... | collective-permute-start | bytes 393224 | tf_op jit(solution)/shard_map/ppermute | solution.py:270
  115.0 131.6 %collective-permute-start.10 = (f32[2,4,64,256]{3,2,1,0:T(8,128)}, f32[2,4,64,256]{3,2,1,0:T(8,128)S(1)}, u32[]{:S(2)}, u32[]{:S(2)}) collective-permute-start(f32[2,4,64,256]{3,2,1,0:T(8,128)} %get-tuple-element.23), channel_id=1, source_target_pairs={{0,8},{8,16},{16,24},{1,9},{9,17},{17,25},{2,10},{10,18},{18,26},{... | collective-permute-start | bytes 1572872 | tf_op jit(solution)/shard_map/ppermute | solution.py:261
  120.4 126.2 %collective-permute-start.11 = (f32[2,4,64,256]{3,2,1,0:T(8,128)}, f32[2,4,64,256]{3,2,1,0:T(8,128)S(1)}, u32[]{:S(2)}, u32[]{:S(2)}) collective-permute-start(f32[2,4,64,256]{3,2,1,0:T(8,128)} %get-tuple-element.24), channel_id=1, source_target_pairs={{8,0},{16,8},{24,16},{9,1},{17,9},{25,17},{10,2},{18,10},{26,18},{... | collective-permute-start | bytes 1572872 | tf_op jit(solution)/shard_map/ppermute | solution.py:261
  121.7 124.9 %collective-permute-start.12 = (f32[4,128,128]{2,1,0:T(8,128)}, f32[4,128,128]{2,1,0:T(8,128)S(1)}, u32[]{:S(2)}, u32[]{:S(2)}) collective-permute-start(f32[4,128,128]{2,1,0:T(8,128)} %get-tuple-element.25), channel_id=1, source_target_pairs={{0,2},{2,4},{4,6},{1,3},{3,5},{5,7},{8,10},{10,12},{12,14},{9,11},... | collective-permute-start | bytes 786440 | tf_op jit(solution)/shard_map/ppermute | solution.py:263
  125.3 121.3 %collective-permute-start.13 = (f32[4,128,128]{2,1,0:T(8,128)S(1)}, f32[4,128,128]{2,1,0:T(8,128)S(1)}, u32[]{:S(2)}, u32[]{:S(2)}) collective-permute-start(f32[4,128,128]{2,1,0:T(8,128)S(1)} %get-tuple-element.26), channel_id=1, source_target_pairs={{2,0},{4,2},{6,4},{3,1},{5,3},{7,5},{10,8},{12,10},{14,12},{11,9},... | collective-permute-start | bytes 786440 | tf_op jit(solution)/shard_map/ppermute | solution.py:263
  126.6 113.7 %collective-permute-start.16 = (f32[4,64,128]{2,1,0:T(8,128)S(1)}, f32[4,64,128]{2,1,0:T(8,128)S(1)}, u32[]{:S(2)}, u32[]{:S(2)}) collective-permute-start(f32[4,64,128]{2,1,0:T(8,128)S(1)} %get-tuple-element.29), channel_id=1, source_target_pairs={{8,2},{10,4},{12,6},{16,10},{18,12},{20,14},{24,18},{26,20},{28,22... | collective-permute-start | bytes 393224 | tf_op jit(solution)/shard_map/ppermute | solution.py:270
  240.3 6.3 %collective-permute-start.17 = (f32[4,64,128]{2,1,0:T(8,128)S(1)}, f32[4,64,128]{2,1,0:T(8,128)S(1)}, u32[]{:S(2)}, u32[]{:S(2)}) collective-permute-start(f32[4,64,128]{2,1,0:T(8,128)S(1)} %get-tuple-element.30), channel_id=1, source_target_pairs={{10,0},{12,2},{14,4},{18,8},{20,10},{22,12},{26,16},{28,18},{30,20... | collective-permute-start | bytes 393224 | tf_op jit(solution)/shard_map/ppermute | solution.py:270
  (9 other events, 7.0 us)
Sparse Core Ops, SparseCore 0:
  115.1 123.6 all-reduce.1

commit v2 on v1

v2 whole, which is shorter than its diff:
```python
import functools

import jax
import jax.numpy as jnp
import ml_dtypes
import numpy as np
from jax import lax
from jax.experimental import pallas as pl
from jax.experimental.pallas import tpu as pltpu
from jax.sharding import PartitionSpec as P

FRESNEL = 12.0
F32 = jnp.float32
BF16 = jnp.bfloat16


def split_table(table):
    high = table.astype(np.float32).astype(ml_dtypes.bfloat16)
    low = (table - high.astype(np.float64)).astype(np.float32).astype(ml_dtypes.bfloat16)
    return high, low


def build_tables(points):
    counter = np.arange(points)
    angles = (counter[:, None] * counter[None, :] % points) * (2.0 * np.pi / points)
    fourier = np.exp(-1j * angles) / np.sqrt(points)
    frequency = np.where(counter < points // 2, counter, counter - points) / points
    transfer = np.exp(-1j * FRESNEL * frequency * frequency)
    prop = (fourier * transfer[None, :]) @ fourier.conj()
    prop = 0.5 * (prop + prop.T)
    tables = []
    for matrix in (prop, fourier):
        re, im = matrix.real, matrix.imag
        right = np.block([[re, im], [-im, re]])
        left = np.block([[re, -im], [im, re]])
        tables.append(np.stack(split_table(right) + split_table(left)))
    return tables


def split(value):
    high = value.astype(BF16)
    low = (value - high.astype(F32)).astype(BF16)
    return high, low


def dot(a, b):
    return jnp.dot(a, b, preferred_element_type=F32)


def dot3(a, b):
    (a_high, a_low), (b_high, b_low) = a, b
    return dot(a_high, b_high) + (dot(a_high, b_low) + dot(a_low, b_high))


def apply_both(table_ref, fields, conj):
    n = fields[0].shape[0]
    first = 2 if conj else 0
    right = (table_ref[first], table_ref[first + 1])
    left = (table_ref[2 - first], table_ref[3 - first])
    mid = dot3(split(jnp.concatenate(fields, axis=0)), right)
    columns = [
        jnp.concatenate([mid[p * n : (p + 1) * n, :n], mid[p * n : (p + 1) * n, n:]], axis=0)
        for p in range(len(fields))
    ]
    out = dot3(left, split(jnp.concatenate(columns, axis=1)))
    return [
        jnp.concatenate([out[:n, p * n : (p + 1) * n], out[n:, p * n : (p + 1) * n]], axis=1)
        for p in range(len(fields))
    ]


def times(a, b):
    n = a.shape[-1] // 2
    ar, ai, br, bi = a[:, :n], a[:, n:], b[:, :n], b[:, n:]
    return jnp.concatenate([ar * br - ai * bi, ar * bi + ai * br], axis=1)


def conj_times(a, b):
    n = a.shape[-1] // 2
    ar, ai, br, bi = a[:, :n], a[:, n:], b[:, :n], b[:, n:]
    return jnp.concatenate([ar * br + ai * bi, ar * bi - ai * br], axis=1)


MESH = pl.DeviceIdType.MESH
SIDES = ((1, 0), (-1, 0), (0, 1), (0, -1), (1, 1), (1, -1), (-1, 1), (-1, -1))


def place():
    return tuple(lax.axis_index(name) for name in ("sx", "sy", "depth"))


def extent():
    return tuple(lax.axis_size(name) for name in ("sx", "sy", "depth"))


def inside(i, j, sizes):
    return (i >= 0) & (i < sizes[0]) & (j >= 0) & (j < sizes[1])


def greet(peers):
    barrier = pltpu.get_barrier_semaphore()
    for exists, device in peers:
        if exists is None:
            pl.semaphore_signal(barrier, inc=1, device_id=device, device_id_type=MESH)
        else:
            @pl.when(exists)
            def _():
                pl.semaphore_signal(barrier, inc=1, device_id=device, device_id_type=MESH)
    count = sum(jnp.int32(1) if exists is None else exists.astype(jnp.int32) for exists, _ in peers)
    pl.semaphore_wait(barrier, count)


def remote(source, target, send_sem, recv_sem, device):
    return pltpu.make_async_remote_copy(
        src_ref=source, dst_ref=target, send_sem=send_sem, recv_sem=recv_sem,
        device_id=device, device_id_type=MESH,
    )


class Rims:
    def __init__(self, sources, targets, send_sems, recv_sems):
        (i, j, d), sizes = place(), extent()
        self.items = []
        for at, (down, right) in enumerate(SIDES):
            copy = remote(sources[at], targets[at], send_sems.at[at], recv_sems.at[at],
                          (i + down, j + right, d))
            goes = inside(i + down, j + right, sizes)
            comes = inside(i - down, j - right, sizes)
            self.items.append((copy, goes, comes, targets[at]))

    def start(self, at):
        copy, goes, _, _ = self.items[at]
        pl.when(goes)(copy.start)

    def wait_recv(self, at):
        copy, _, comes, target = self.items[at]
        pl.when(comes)(copy.wait_recv)

        @pl.when(jnp.logical_not(comes))
        def _():
            target[...] = jnp.zeros_like(target)

    def wait_send(self, at):
        copy, goes, _, _ = self.items[at]
        pl.when(goes)(copy.wait_send)


def window_place(off_ref, p, n, cols):
    row = off_ref[p, 0] + n // 2
    down = lax.rem(row, 8)
    row = pl.multiple_of(row - down, 8)
    col = off_ref[p, 1] + n
    block = jnp.minimum(col // n, (cols + n) // n - 1)
    start = pl.multiple_of(block * n, n)
    return row, down, start, col - start


def rim_rows(b, rows):
    return ((0, b), (b, rows), (b + rows, b))


def halo_kernel(own_ref, *refs):
    outs, (first, last, *bufs), (send_sems, recv_sems) = refs[:8], refs[8:18], refs[18:]
    (i, j, d), sizes = place(), extent()
    slabs, rows, cols = own_ref.shape[1:]
    n = first.shape[-1]
    b = n // 2
    lane = lax.broadcasted_iota(jnp.int32, (1, n), 1)
    for k in range(slabs):
        re, im = (own_ref[part, k, :, :n] for part in range(2))
        first[k] = jnp.where(lane < b, re, pltpu.roll(im, b, 1))
        re, im = (own_ref[part, k, :, cols - n :] for part in range(2))
        last[k] = jnp.where(lane < b, pltpu.roll(re, b, 1), im)
    greet([(inside(i + y, j + x, sizes), (i + y, j + x, d)) for y, x in SIDES])
    low, high = pl.ds(rows - b, b), pl.ds(0, b)
    rims = Rims(
        [own_ref.at[:, :, low], own_ref.at[:, :, high], last, first,
         last.at[:, low], first.at[:, low], last.at[:, high], first.at[:, high]],
        bufs, send_sems, recv_sems,
    )
    for at in range(len(SIDES)):
        rims.start(at)
    for at in range(len(SIDES)):
        rims.wait_recv(at)
        outs[at][...] = bufs[at][...]
    for at in range(len(SIDES)):
        rims.wait_send(at)


def cut_kernel(off_ref, shift_ref, own_ref, patterns_ref, up, down, left, right, ul, ur, dl, dr,
               factor, measured, ext):
    positions, slabs, n, _ = factor.shape
    rows, cols = own_ref.shape[2:]
    b = n // 2
    for k in range(slabs):
        for part in range(2):
            ext[part, k, b : b + rows, n : n + cols] = own_ref[part, k]
            ext[part, k, :b, n : n + cols] = up[part, k]
            ext[part, k, b + rows : n + rows, n : n + cols] = down[part, k]
            for (x_ref, y_ref), (at, size) in zip(((ul, ur), (left, right), (dl, dr)), rim_rows(b, rows)):
                x, y = x_ref[k], y_ref[k]
                if part == 0:
                    x = pltpu.roll(x, b, 1)
                else:
                    y = pltpu.roll(y, b, 1)
                ext[part, k, at : at + size, :n] = x
                ext[part, k, at : at + size, n + cols :] = y
    for p in range(positions):
        value = pltpu.roll(patterns_ref[p], lax.rem(2 * n - shift_ref[p, 0], n), 0)
        measured[p] = pltpu.roll(value, lax.rem(2 * n - shift_ref[p, 1], n), 1)
        row, off, start, shift = window_place(off_ref, p, n, cols)
        for k in range(slabs):
            parts = []
            for part in range(2):
                wide = ext[part, k, pl.ds(row, n + 8), pl.ds(start, 2 * n)]
                wide = pltpu.roll(wide, lax.rem(2 * n - shift, 2 * n), 1)[:, :n]
                parts.append(pltpu.roll(wide, lax.rem(n + 8 - off, n + 8), 0)[:n])
            factor[p, k] = jnp.concatenate([1.0 + parts[0], parts[1]], axis=1)


def wave_kernel(group_size, factor, probe_ref, measured, prop_ref, fourier_ref, piece_ref, red_ref,
                incident, wave, arrived, grad, returned, error, error_in,
                wave_send, wave_recv, grad_send, grad_recv, error_send, error_recv):
    (i, j, d), sizes = place(), extent()
    depth = sizes[2]
    positions, slabs, n, _ = factor.shape
    final = depth - 1
    greet([(None, (i, j, lax.rem(d + step, depth))) for step in range(1, depth)])
    error[...] = jnp.zeros_like(error)

    def wave_copy(p):
        return remote(wave.at[p], arrived.at[p], wave_send.at[p], wave_recv.at[p], (i, j, d + 1))

    def grad_copy(p):
        return remote(grad.at[p], returned.at[p], grad_send.at[p], grad_recv.at[p], (i, j, d - 1))

    error_copy = remote(error, error_in, error_send, error_recv, (i, j, 0))

    def backward(group):
        @pl.loop(0, slabs)
        def _(step):
            k = slabs - 1 - step
            for p, value in zip(group, apply_both(prop_ref, [grad[p] for p in group], True)):
                piece_ref[p, k] = conj_times(incident[p, k], value)
                grad[p] = conj_times(factor[p, k], value)

    groups = [list(range(g, g + group_size)) for g in range(0, positions, group_size)]

    for group in groups:
        @pl.when(d == 0)
        def _():
            for p in group:
                wave[p] = probe_ref[...]

        @pl.when(d > 0)
        def _():
            for p in group:
                wave_copy(p).wait_recv()
                wave[p] = arrived[p]

        @pl.loop(0, slabs)
        def _(k):
            values = [wave[p] for p in group]
            for p, value in zip(group, values):
                incident[p, k] = value
            values = [times(value, factor[p, k]) for p, value in zip(group, values)]
            for p, value in zip(group, apply_both(prop_ref, values, False)):
                wave[p] = value

        @pl.when(d < final)
        def _():
            for p in group:
                wave_copy(p).start()

        @pl.when(d == final)
        def _():
            fars = apply_both(fourier_ref, [wave[p] for p in group], False)
            values = []
            for p, far in zip(group, fars):
                fr, fi = far[:, :n], far[:, n:]
                residual = fr * fr + fi * fi - measured[p]
                error[:, :n] += jnp.sum((residual * residual).reshape(n // 8, 8, n), axis=0)
                residual = 2.0 * residual
                values.append(jnp.concatenate([residual * fr, residual * fi], axis=1))
            for p, value in zip(group, apply_both(fourier_ref, values, True)):
                grad[p] = value
            backward(group)
            for p in group:
                grad_copy(p).start()

    @pl.when(d == final)
    def _():
        error_copy.start()

    @pl.when(d < final)
    def _():
        for group in groups:
            for p in group:
                grad_copy_in(p, grad, returned, grad_send, grad_recv, (i, j, d + 1)).wait_recv()
                grad[p] = returned[p]
            backward(group)

            @pl.when(d > 0)
            def _():
                for p in group:
                    grad_copy(p).start()

    @pl.when(d == 0)
    def _():
        error_copy_in = remote(error, error_in, error_send, error_recv, (i, j, final))
        error_copy_in.wait_recv()
        total = grad[0]
        for p in range(1, positions):
            total = total + grad[p]
        height = n // red_ref.shape[0]
        for part in range(red_ref.shape[0]):
            red_ref[part, :height] = total[part * height : (part + 1) * height]
            red_ref[part, height:] = error_in[...]

    @pl.when(d > 0)
    def _():
        red_ref[...] = jnp.zeros_like(red_ref)
        for p in range(positions):
            grad_copy(p).wait_send()

    @pl.when(d == final)
    def _():
        error_copy.wait_send()

    @pl.when(d < final)
    def _():
        for p in range(positions):
            wave_copy(p).wait_send()


def grad_copy_in(p, grad, returned, grad_send, grad_recv, device):
    return remote(grad.at[p], returned.at[p], grad_send.at[p], grad_recv.at[p], device)


def scatter_kernel(off_ref, piece_ref, center, up, down, left_ref, right_ref, ul_ref, ur_ref, dl_ref,
                   dr_ref, ext):
    positions, slabs, n, _ = piece_ref.shape
    rows, cols = center.shape[2:]
    b = n // 2
    ext[...] = jnp.zeros_like(ext)
    for p in range(positions):
        row, off, start, shift = window_place(off_ref, p, n, cols)
        for k in range(slabs):
            for part in range(2):
                value = piece_ref[p, k, :, part * n : (part + 1) * n]
                value = jnp.concatenate([value, jnp.zeros((8, n), F32)], axis=0)
                value = pltpu.roll(value, off, 0)
                wide = jnp.concatenate([value, jnp.zeros_like(value)], axis=1)
                ext[part, k, pl.ds(row, n + 8), pl.ds(start, 2 * n)] += pltpu.roll(wide, lax.rem(shift, 2 * n), 1)
    lane = lax.broadcasted_iota(jnp.int32, (1, n), 1)
    for k in range(slabs):
        for part in range(2):
            center[part, k] = ext[part, k, b : b + rows, n : n + cols]
            up[part, k] = ext[part, k, :b, n : n + cols]
            down[part, k] = ext[part, k, b + rows : n + rows, n : n + cols]
        for left, right, (at, size) in zip(
            (ul_ref, left_ref, dl_ref), (ur_ref, right_ref, dr_ref), rim_rows(b, rows)
        ):
            re, im = (ext[part, k, at : at + size, :n] for part in range(2))
            left[k] = jnp.where(lane < b, pltpu.roll(re, b, 1), im)
            re, im = (ext[part, k, at : at + size, n + cols :] for part in range(2))
            right[k] = jnp.where(lane < b, re, pltpu.roll(im, b, 1))


def fold_kernel(center, to_up, to_down, to_left, to_right, to_ul, to_ur, to_dl, to_dr, red_ref,
                out, total_ref, up, down, left, right, ul, ur, dl, dr, part_in, column_in, mine,
                whole, send_sems, recv_sems, part_send, part_recv, column_send, column_recv,
                whole_send, whole_recv):
    (i, j, d), sizes = place(), extent()
    n_sx, n_sy, depth = sizes
    slabs, rows, cols = center.shape[1:]
    b = up.shape[2]
    n = 2 * b
    across = [lax.rem(i + step, n_sx) for step in range(1, n_sx)]
    along = [lax.rem(j + step, n_sy) for step in range(1, n_sy)]
    peers = [(None, (x, j, d)) for x in across] + [(None, (i, y, d)) for y in along]
    peers += [(inside(i + y, j + x, sizes), (i + y, j + x, d)) for y, x in SIDES if y and x]
    others = [(x, lax.rem(d + step, depth)) for step in range(1, depth) for x in range(n_sx)]
    peers += [(None, (x, j, z)) for x, z in others]
    greet(peers)
    rims = Rims([to_down, to_up, to_right, to_left, to_dr, to_dl, to_ur, to_ul],
                [up, down, left, right, ul, ur, dl, dr], send_sems, recv_sems)

    parts = [
        remote(red_ref.at[x], part_in.at[step], part_send.at[step], part_recv.at[step], (x, j, d))
        for step, x in enumerate(across)
    ]
    columns = [
        remote(mine, column_in.at[j], column_send.at[step], column_recv.at[j], (i, y, d))
        for step, y in enumerate(along)
    ]
    wholes = [
        remote(whole.at[i], whole.at[i], whole_send.at[step], whole_recv.at[i], (x, j, z))
        for step, (x, z) in enumerate([(x, d) for x in across] + others)
    ]

    @pl.when(d == 0)
    def _():
        for copy in parts:
            copy.start()

    rims.start(0)
    rims.start(1)

    @pl.when(d == 0)
    def _():
        value = red_ref[i]
        for step, copy in enumerate(parts):
            copy.wait_recv()
            value = value + part_in[step]
        mine[...] = value
        for copy in columns:
            copy.start()

    for at in range(2, len(SIDES)):
        rims.start(at)
    for k in range(slabs):
        for part in range(2):
            out[part, k] = center[part, k]

    @pl.when(d == 0)
    def _():
        for step in range(1, n_sy):
            y = lax.rem(j + n_sy - step, n_sy)
            remote(mine, column_in.at[y], column_send.at[step - 1], column_recv.at[y], (i, y, d)).wait_recv()
        column_in[j] = mine[...]
        value = column_in[0]
        for y in range(1, n_sy):
            value = value + column_in[y]
        whole[i] = value
        for copy in wholes:
            copy.start()

    for at in range(2):
        rims.wait_recv(at)
    for k in range(slabs):
        for part in range(2):
            out[part, k, :b] += up[part, k]
            out[part, k, rows - b :] += down[part, k]
    for at in range(2, len(SIDES)):
        rims.wait_recv(at)
    lane = lax.broadcasted_iota(jnp.int32, (1, n), 1)
    for k in range(slabs):
        for part in range(2):
            for x_ref, y_ref, at, size in ((left, right, 0, rows), (ul, ur, 0, b), (dl, dr, rows - b, b)):
                x, y = x_ref[k], y_ref[k]
                if part == 1:
                    x = pltpu.roll(x, b, 1)
                else:
                    y = pltpu.roll(y, b, 1)
                out[part, k, at : at + size, :n] += jnp.where(lane < b, x, 0.0)
                out[part, k, at : at + size, cols - n :] += jnp.where(lane < b, 0.0, y)

    def whole_arrives(x):
        remote(whole.at[x], whole.at[x], whole_send.at[0], whole_recv.at[x], (x, j, d)).wait_recv()

    for x in across:
        whole_arrives(x)
    pl.when(d > 0)(lambda: whole_arrives(i))
    for x in range(n_sx):
        total_ref[x] = whole[x]

    @pl.when(d == 0)
    def _():
        for copy in parts + columns + wholes:
            copy.wait_send()

    for at in range(len(SIDES)):
        rims.wait_send(at)


VMEM = pl.BlockSpec(memory_space=pltpu.VMEM)
SMEM = pl.BlockSpec(memory_space=pltpu.SMEM)


def call(kernel, args, outs, smem=0, scratch=(), sems=(), collective=None):
    params = dict(vmem_limit_bytes=48 * 1024 * 1024)
    if collective is not None:
        params.update(collective_id=collective, has_side_effects=True)
    return pl.pallas_call(
        kernel,
        out_shape=[jax.ShapeDtypeStruct(shape, F32) for shape in outs],
        in_specs=[SMEM] * smem + [VMEM] * (len(args) - smem),
        out_specs=[VMEM] * len(outs),
        scratch_shapes=[pltpu.VMEM(shape, F32) for shape in scratch]
        + [pltpu.SemaphoreType.DMA(shape) if shape else pltpu.SemaphoreType.DMA for shape in sems],
        compiler_params=pltpu.CompilerParams(**params),
    )(*args)


def local(probe_wave, transmission, scan_offsets, pattern_shifts, patterns):
    n = probe_wave.shape[-1]
    b = n // 2
    _, slabs, rows, cols = transmission.shape
    prop_table, fourier_table = (jnp.asarray(t) for t in build_tables(n))
    offsets = scan_offsets.reshape(-1, 2)
    shifts = pattern_shifts.reshape(-1, 2)
    measured = patterns.reshape(-1, n, n)
    positions = offsets.shape[0]
    n_sx, n_sy, depth = extent()
    probe = jnp.concatenate([probe_wave[0], probe_wave[1]], axis=-1)

    wave_shape = (positions, n, 2 * n)
    store_shape = (positions, slabs, n, 2 * n)
    ext_shape = (2, slabs, rows + n + 8, cols + 2 * n)
    side_shape, edge_shape, corner_shape = (slabs, rows, n), (2, slabs, b, cols), (slabs, b, n)
    rim_shapes = [edge_shape] * 2 + [side_shape] * 2 + [corner_shape] * 4
    chunk = (n // n_sx + 8, 2 * n)
    sides = (len(SIDES),)
    rims = call(halo_kernel, [transmission], rim_shapes, scratch=[side_shape] * 2 + rim_shapes,
                sems=[sides] * 2, collective=0)
    factor, moved = call(
        cut_kernel, [offsets, shifts, transmission, measured, *rims],
        [store_shape, (positions, n, n)], smem=2, scratch=[ext_shape],
    )
    pieces, red = call(
        functools.partial(wave_kernel, 2 if positions % 2 == 0 else 1),
        [factor, probe, moved, prop_table, fourier_table], [store_shape, (n_sx, *chunk)],
        scratch=[store_shape] + [wave_shape] * 4 + [(8, 2 * n)] * 2,
        sems=[(positions,)] * 4 + [()] * 2, collective=2,
    )
    rims = call(scatter_kernel, [offsets, pieces], [transmission.shape, *rim_shapes], smem=1, scratch=[ext_shape])
    transmission_grad, totals = call(
        fold_kernel, [*rims, red], [transmission.shape, (n_sx, *chunk)],
        scratch=rim_shapes + [(n_sx - 1, *chunk), (n_sy, *chunk), chunk, (n_sx, *chunk)],
        sems=[sides] * 2 + [(n_sx - 1,)] * 2 + [(n_sy - 1,), (n_sy,), (n_sx * depth - 1,), (n_sx,)], collective=1,
    )
    all_positions = positions * n_sx * n_sy
    summed = totals[:, : n // n_sx].reshape(n, 2 * n)
    probe_grad = jnp.stack([summed[:, :n], summed[:, n:]]) / all_positions
    mean_error = 0.5 * jnp.sum(totals[0, n // n_sx :, :n]) / (all_positions * n * n)
    return (transmission_grad, probe_grad, mean_error)


def solution(mesh):
    in_specs = (
        P(),
        P(None, "depth", "sx", "sy"),
        P("sx", "sy", None, None),
        P("sx", "sy", None, None),
        P("sx", "sy", None, None, None),
    )
    out_specs = (P(None, "depth", "sx", "sy"), P(), P())
    return jax.shard_map(local, mesh=mesh, in_specs=in_specs, out_specs=out_specs, check_vma=False)
```

time: 260 us -> 88 us (0.34); the launches traced: 256 us -> 87.1 us
  waiting for transfers between devices: 144 us -> 0 us
  Pallas kernels: 27.6 us -> 77.7 us
  starting transfers between devices: 44.4 us -> 0 us
  between operations: 16.2 us -> 2.51 us
  local copies, waits for them, and re-layouts: 16.7 us -> 5.57 us
  other arithmetic: 7.14 us -> 1.28 us
    psum x1 -> x0, waiting for transfers between devices: 111 us -> none  [local(): lax.psum(jnp.concatenate([probe_part, jnp.concatenate([error_part, error_...]
    pallas_call x5, Pallas kernels: 27.6 us -> 77.7 us  [call(): pl.pallas_call(kernel, out_shape=[jax.ShapeDtypeStruct(shape, F32) for sh...]
    ppermute x18 -> x0, starting transfers between devices: 44.4 us -> none  [the longest x4 15.7 us: shifted(): lax.ppermute(value, 'sx', [(i, i + down) for i in range(rows) if 0 <= i +...]
    ppermute x18 -> x0, waiting for transfers between devices: 32.4 us -> none  [the longest x1 14.8 us: local(): incoming = lax.ppermute(grad_start, 'depth', backward_pairs)]
    unnamed x44 -> x9, local copies, waits for them, and re-layouts: 11.3 us -> 3.14 us
    concatenate x6 -> x1, other arithmetic: 3.23 us -> 0.01 us  [local(): probe = jnp.concatenate([probe_wave[0], probe_wave[1]], axis=-1)]
  transfers between devices with their start and end apart: 19 -> 0, of which waited for: 6 -> 0; matrix products, arithmetic and copies ran while one was open for 3% -> 0% of each run, Pallas kernels for 0% -> 0%
where the time goes in v2:
time: 88 us; the launch traced here: 87.1 us
  Pallas kernels  77.7 us (88%)
  local copies, waits for them, and re-layouts  5.57 us (6%)
  between operations  2.51 us (3%)
  other arithmetic  1.28 us (1%)
    pallas_call x5, Pallas kernels, call(): pl.pallas_call(kernel, out_shape=[jax.ShapeDtypeStruct(shape, F32) for sh...  77.7 us
    unnamed x9, local copies, waits for them, and re-layouts  3.14 us

profile of v2, /device:TPU:0, one launch (start us, length us, event | category | flops | bytes accessed | tf_op | source)
XLA Modules:
  0.0 87.1 jit_solution(3651212149081568064)
XLA Ops:
  0.6 0.8 copy.12.off_ref
  1.4 0.8 copy.11.shift_ref
  2.2 0.9 %slice_bitcast_fusion.3 = (f32[128,128]{1,0:T(8,128)S(1)}, f32[128,128]{1,0:T(8,128)S(1)}) fusion(f32[2,128,128]{2,1,0:T(8,128)} %param.7), kind=kLoop, calls=%fused_computation.5 | loop fusion | bytes 262144 | tf_op jit(solution)/shard_map/squeeze | solution.py:506
  3.1 0.0 copy-start
  3.1 1.2 %copy-done = f32[2,4,128,256]{3,2,1,0:T(8,128)S(1)} copy-done((f32[2,4,128,256]{3,2,1,0:T(8,128)S(1)}, f32[2,4,128,256]{3,2,1,0:T(8,128)}, u32[]{:S(2)}) %copy-start) | copy-done | bytes 1048600
  4.3 0.0 copy-start.1
  4.3 0.0 copy-start.2
  4.3 16.3 %shard_map.94 = (f32[2,4,64,256]{3,2,1,0:T(8,128)S(1)}, f32[2,4,64,256]{3,2,1,0:T(8,128)S(1)}, f32[4,128,128]{2,1,0:T(8,128)S(1)}, f32[4,128,128]{2,1,0:T(8,128)...) custom-call(f32[2,4,128,256]{3,2,1,0:T(8,128)S(1)} %copy-done), custom_call_target="tpu_custom_call" | custom-call | tf_op jit(solution)/shard_map/pallas_call | solution.py:485
  20.7 0.0 copy-start.3
  20.7 0.9 %copy-done.3 = f32[1,1,4,128,128]{4,3,2,1,0:T(8,128)S(1)} copy-done((f32[1,1,4,128,128]{4,3,2,1,0:T(8,128)S(1)}, f32[1,1,4,128,128]{4,3,2,1,0:T(8,128)}, u32[]{:S(2)}) %copy-start.3) | copy-done | bytes 262168
  21.6 2.4 %shard_map.95 = (f32[4,4,128,256]{3,2,1,0:T(8,128)S(1)}, f32[4,128,128]{2,1,0:T(8,128)S(1)}) custom-call(s32[4,2]{1,0:T(4,128)S(1)} %copy.12.off_ref, s32[4,2]{1,0:T(4,128)S(1)} %copy.11.shift_ref, f32[2,4,128,256]{3,2,1,0:T(8,128)S(1)} %copy-done, f32[4,128,128]{2,1,0:T(8,128)S(1)} %bitcast.12, f32[2,4,64,256]{3,2,1,0:T(8,128)S(1)} %get-tuple-element.26.up, ...), custom_call_target="tpu_custom_call" | custom-call | tf_op jit(solution)/shard_map/pallas_call | solution.py:485
  24.0 0.0 copy-done.1
  24.0 0.0 copy-done.2
  24.1 35.8 %shard_map.96 = (f32[4,4,128,256]{3,2,1,0:T(8,128)S(1)}, f32[4,40,256]{2,1,0:T(8,128)S(1)}) custom-call(f32[4,4,128,256]{3,2,1,0:T(8,128)S(1)} %get-tuple-element.34.factor, f32[128,256]{1,0:T(8,128)S(1)} %pad_maximum_fusion.probe_ref, f32[4,128,128]{2,1,0:T(8,128)S(1)} %get-tuple-element.35.measured, bf16[4,256,256]{2,1,0:T(8,128)(2,1)S(1)} %copy-done.2, ...), custom_call_target="tpu_custom_call" | custom-call | tf_op jit(solution)/shard_map/pallas_call | solution.py:485
  59.8 2.3 %shard_map.97 = (f32[2,4,128,256]{3,2,1,0:T(8,128)S(1)}, f32[2,4,64,256]{3,2,1,0:T(8,128)S(1)}, f32[2,4,64,256]{3,2,1,0:T(8,128)S(1)}, f32[4,128,128]{2,1,0:T(8,...) custom-call(s32[4,2]{1,0:T(4,128)S(1)} %copy.12.off_ref, ...), custom_call_target="tpu_custom_call" | custom-call | tf_op jit(solution)/shard_map/pallas_call | solution.py:485
  62.1 20.9 %shard_map.98 = (f32[2,4,128,256]{3,2,1,0:T(8,128)S(1)}, f32[4,40,256]{2,1,0:T(8,128)S(1)}) custom-call(f32[2,4,128,256]{3,2,1,0:T(8,128)S(1)} %get-tuple-element.37.center, f32[2,4,64,256]{3,2,1,0:T(8,128)S(1)} %get-tuple-element.38.to_up, f32[2,4,64,256]{3,2,1,0:T(8,128)S(1)} %get-tuple-element.39.to_down, f32[4,128,128]{2,1,0:T(8,128)S(1)} %get-tuple-element.40.to_left, ...), custom_call_target="tpu_custom_call" | custom-call | tf_op jit(solution)/shard_map/pallas_call | solution.py:485
  83.1 0.6 slice_reduce_fusion
  84.3 0.7 maximum_multiply_fusion
  85.0 1.0 %copy.14 = f32[2,4,128,256]{3,2,1,0:T(8,128)} copy(f32[2,4,128,256]{3,2,1,0:T(8,128)S(1)} %get-tuple-element.56) | data formatting | bytes 2097152
  (3 shorter events, 0.0 us)
Async XLA Ops:
  3.1 1.2 %copy-start = (f32[2,4,128,256]{3,2,1,0:T(8,128)S(1)}, f32[2,4,128,256]{3,2,1,0:T(8,128)}, u32[]{:S(2)}) copy-start(f32[2,4,128,256]{3,2,1,0:T(8,128)} %own_ref.3) | copy-start | bytes 3145732
  4.3 19.7 %copy-start.1 = (bf16[4,256,256]{2,1,0:T(8,128)(2,1)S(1)}, bf16[4,256,256]{2,1,0:T(8,128)(2,1)}, u32[]{:S(2)}) copy-start(bf16[4,256,256]{2,1,0:T(8,128)(2,1)} %constant.15.clone.fourier_ref) | copy-start | bytes 1572868
  4.3 19.8 %copy-start.2 = (bf16[4,256,256]{2,1,0:T(8,128)(2,1)S(1)}, bf16[4,256,256]{2,1,0:T(8,128)(2,1)}, u32[]{:S(2)}) copy-start(bf16[4,256,256]{2,1,0:T(8,128)(2,1)} %constant.14.clone.prop_ref) | copy-start | bytes 1572868
  20.7 1.0 %copy-start.3 = (f32[1,1,4,128,128]{4,3,2,1,0:T(8,128)S(1)}, f32[1,1,4,128,128]{4,3,2,1,0:T(8,128)}, u32[]{:S(2)}) copy-start(f32[1,1,4,128,128]{4,3,2,1,0:T(8,128)} %param.11) | copy-start | bytes 786436

commit v3 on v2

--- a/solution.py
+++ b/solution.py
@@ -519,7 +519,7 @@
         [store_shape, (positions, n, n)], smem=2, scratch=[ext_shape],
     )
     pieces, red = call(
-        functools.partial(wave_kernel, 2 if positions % 2 == 0 else 1),
+        functools.partial(wave_kernel, 1),
         [factor, probe, moved, prop_table, fourier_table], [store_shape, (n_sx, *chunk)],
         scratch=[store_shape] + [wave_shape] * 4 + [(8, 2 * n)] * 2,
         sems=[(positions,)] * 4 + [()] * 2, collective=2,

time: 88 us -> 88.7 us (level)
  no operation moved by 1% of the time
where the time goes in v3:
time: 88.7 us; the launch traced here: 87.6 us
  Pallas kernels  78.2 us (88%)
  local copies, waits for them, and re-layouts  5.57 us (6%)
  between operations  2.51 us (3%)
  other arithmetic  1.28 us (1%)
    pallas_call x5, Pallas kernels, call(): pl.pallas_call(kernel, out_shape=[jax.ShapeDtypeStruct(shape, F32) for sh...  78.2 us
    unnamed x9, local copies, waits for them, and re-layouts  3.14 us

profile of v3, /device:TPU:0, one launch (start us, length us, event | category | flops | bytes accessed | tf_op | source)
XLA Modules:
  0.0 87.6 jit_solution(17972924507737396656)
XLA Ops:
  0.6 0.8 copy.12.off_ref
  1.4 0.8 copy.11.shift_ref
  2.2 0.9 %slice_bitcast_fusion.3 = (f32[128,128]{1,0:T(8,128)S(1)}, f32[128,128]{1,0:T(8,128)S(1)}) fusion(f32[2,128,128]{2,1,0:T(8,128)} %param.7), kind=kLoop, calls=%fused_computation.5 | loop fusion | bytes 262144 | tf_op jit(solution)/shard_map/squeeze | solution.py:506
  3.1 0.0 copy-start
  3.1 1.2 %copy-done = f32[2,4,128,256]{3,2,1,0:T(8,128)S(1)} copy-done((f32[2,4,128,256]{3,2,1,0:T(8,128)S(1)}, f32[2,4,128,256]{3,2,1,0:T(8,128)}, u32[]{:S(2)}) %copy-start) | copy-done | bytes 1048600
  4.3 0.0 copy-start.1
  4.3 0.0 copy-start.2
  4.3 16.3 %shard_map.94 = (f32[2,4,64,256]{3,2,1,0:T(8,128)S(1)}, f32[2,4,64,256]{3,2,1,0:T(8,128)S(1)}, f32[4,128,128]{2,1,0:T(8,128)S(1)}, f32[4,128,128]{2,1,0:T(8,128)...) custom-call(f32[2,4,128,256]{3,2,1,0:T(8,128)S(1)} %copy-done), custom_call_target="tpu_custom_call" | custom-call | tf_op jit(solution)/shard_map/pallas_call | solution.py:485
  20.7 0.0 copy-start.3
  20.7 0.9 %copy-done.3 = f32[1,1,4,128,128]{4,3,2,1,0:T(8,128)S(1)} copy-done((f32[1,1,4,128,128]{4,3,2,1,0:T(8,128)S(1)}, f32[1,1,4,128,128]{4,3,2,1,0:T(8,128)}, u32[]{:S(2)}) %copy-start.3) | copy-done | bytes 262168
  21.6 2.4 %shard_map.95 = (f32[4,4,128,256]{3,2,1,0:T(8,128)S(1)}, f32[4,128,128]{2,1,0:T(8,128)S(1)}) custom-call(s32[4,2]{1,0:T(4,128)S(1)} %copy.12.off_ref, s32[4,2]{1,0:T(4,128)S(1)} %copy.11.shift_ref, f32[2,4,128,256]{3,2,1,0:T(8,128)S(1)} %copy-done, f32[4,128,128]{2,1,0:T(8,128)S(1)} %bitcast.12, f32[2,4,64,256]{3,2,1,0:T(8,128)S(1)} %get-tuple-element.26.up, ...), custom_call_target="tpu_custom_call" | custom-call | tf_op jit(solution)/shard_map/pallas_call | solution.py:485
  24.0 0.0 copy-done.1
  24.0 0.0 copy-done.2
  24.1 36.6 %shard_map.96 = (f32[4,4,128,256]{3,2,1,0:T(8,128)S(1)}, f32[4,40,256]{2,1,0:T(8,128)S(1)}) custom-call(f32[4,4,128,256]{3,2,1,0:T(8,128)S(1)} %get-tuple-element.34.factor, f32[128,256]{1,0:T(8,128)S(1)} %pad_maximum_fusion.probe_ref, f32[4,128,128]{2,1,0:T(8,128)S(1)} %get-tuple-element.35.measured, bf16[4,256,256]{2,1,0:T(8,128)(2,1)S(1)} %copy-done.2, ...), custom_call_target="tpu_custom_call" | custom-call | tf_op jit(solution)/shard_map/pallas_call | solution.py:485
  60.7 2.3 %shard_map.97 = (f32[2,4,128,256]{3,2,1,0:T(8,128)S(1)}, f32[2,4,64,256]{3,2,1,0:T(8,128)S(1)}, f32[2,4,64,256]{3,2,1,0:T(8,128)S(1)}, f32[4,128,128]{2,1,0:T(8,...) custom-call(s32[4,2]{1,0:T(4,128)S(1)} %copy.12.off_ref, ...), custom_call_target="tpu_custom_call" | custom-call | tf_op jit(solution)/shard_map/pallas_call | solution.py:485
  63.0 20.5 %shard_map.98 = (f32[2,4,128,256]{3,2,1,0:T(8,128)S(1)}, f32[4,40,256]{2,1,0:T(8,128)S(1)}) custom-call(f32[2,4,128,256]{3,2,1,0:T(8,128)S(1)} %get-tuple-element.37.center, f32[2,4,64,256]{3,2,1,0:T(8,128)S(1)} %get-tuple-element.38.to_up, f32[2,4,64,256]{3,2,1,0:T(8,128)S(1)} %get-tuple-element.39.to_down, f32[4,128,128]{2,1,0:T(8,128)S(1)} %get-tuple-element.40.to_left, ...), custom_call_target="tpu_custom_call" | custom-call | tf_op jit(solution)/shard_map/pallas_call | solution.py:485
  83.5 0.6 slice_reduce_fusion
  84.8 0.7 maximum_multiply_fusion
  85.5 1.0 %copy.14 = f32[2,4,128,256]{3,2,1,0:T(8,128)} copy(f32[2,4,128,256]{3,2,1,0:T(8,128)S(1)} %get-tuple-element.56) | data formatting | bytes 2097152
  (3 shorter events, 0.0 us)
Async XLA Ops:
  3.1 1.2 %copy-start = (f32[2,4,128,256]{3,2,1,0:T(8,128)S(1)}, f32[2,4,128,256]{3,2,1,0:T(8,128)}, u32[]{:S(2)}) copy-start(f32[2,4,128,256]{3,2,1,0:T(8,128)} %own_ref.3) | copy-start | bytes 3145732
  4.3 19.7 %copy-start.1 = (bf16[4,256,256]{2,1,0:T(8,128)(2,1)S(1)}, bf16[4,256,256]{2,1,0:T(8,128)(2,1)}, u32[]{:S(2)}) copy-start(bf16[4,256,256]{2,1,0:T(8,128)(2,1)} %constant.15.clone.fourier_ref) | copy-start | bytes 1572868
  4.3 19.7 %copy-start.2 = (bf16[4,256,256]{2,1,0:T(8,128)(2,1)S(1)}, bf16[4,256,256]{2,1,0:T(8,128)(2,1)}, u32[]{:S(2)}) copy-start(bf16[4,256,256]{2,1,0:T(8,128)(2,1)} %constant.14.clone.prop_ref) | copy-start | bytes 1572868
  20.7 1.0 %copy-start.3 = (f32[1,1,4,128,128]{4,3,2,1,0:T(8,128)S(1)}, f32[1,1,4,128,128]{4,3,2,1,0:T(8,128)}, u32[]{:S(2)}) copy-start(f32[1,1,4,128,128]{4,3,2,1,0:T(8,128)} %param.11) | copy-start | bytes 786436
